TPU v7x, 512 devices: a whole 4x8x8 slice. The times are simulated.
512 devices in a mesh: op: 8 (over z), sec: 64 (over x, y, core).
Axes of the slice: x: 4, y: 8, z: 8, core: 2. Of those that a mesh axis runs over, the one named last changes fastest.
Arguments:
- psi_first: bfloat16 [768, 128, 128], P('sec'), may hold values from -6 to 6
- psi_second: bfloat16 [768, 128, 128], P('sec'), may hold values from -6 to 6
- left_env: bfloat16 [40, 128, 128, 128], P('op', 'sec'), may hold values from -0.078125 to 0.078125
- right_env: bfloat16 [40, 6, 128, 128], P('op'), may hold values from -0.5 to 0.5
- links: int32 [8, 768], P('op'), may hold values from 0 to 767, as said below
Outputs:
- applied_first: bfloat16 [768, 128, 128], P('sec')
- applied_second: bfloat16 [768, 128, 128], P('sec')
Inputs may be any that keep to these rules, and one draw needn't show every extreme that they name: Within each block of links formed by one index of op and one index of sec (8 // 8 groups by 12 tiles), at most 1 entries name tiles held by any one index of sec, and exactly 1 entries name tiles of some one index.
All inputs are finite; a program needn't handle non-finite values.
Results may differ from a plain program's by a relative error of at most 0.0049.
Values may be sent and summed in bfloat16 or wider, within the bound.
No kernel may reach another device: no remote copies, remote signals or barrier semaphores. Data moves between devices by JAX's collectives and lax.ppermute only.
A program may use at most 64 MiB of HBM per device.

v0:
```python
import jax
import jax.numpy as jnp
from jax import lax
from jax.sharding import PartitionSpec as P


def shards(psi_first, psi_second, left_env, right_env, links):
    peer_count = lax.axis_size("sec")
    myself = lax.axis_index("sec")
    tile_count = psi_first.shape[0]
    tile_width = psi_first.shape[1]
    term_count = left_env.shape[0]
    group_count = links.shape[0]
    group_terms = term_count // group_count
    entry_count = group_count * tile_count
    left_count = left_env.shape[1]
    right_count = right_env.shape[1]
    capacity = max(1, (entry_count + peer_count - 1) // peer_count)
    wanted = lax.dynamic_slice_in_dim(links, myself * tile_count, tile_count, 1).reshape(
        entry_count
    )
    holder = wanted // tile_count
    before = jnp.arange(entry_count)[None, :] < jnp.arange(entry_count)[:, None]
    position = jnp.sum((holder[None, :] == holder[:, None]) & before, axis=1)
    requests = (
        links.reshape(group_count, peer_count, tile_count)
        .transpose(1, 0, 2)
        .reshape(peer_count, entry_count)
    )
    request_holder = requests // tile_count
    request_position = jnp.sum(
        (request_holder[:, None, :] == request_holder[:, :, None]) & before[None], axis=2
    )
    matching = (request_holder[:, None, :] == myself) & (
        request_position[:, None, :] == jnp.arange(capacity)[None, :, None]
    )
    chosen = jnp.sum(jnp.where(matching, requests[:, None, :] % tile_count, 0), axis=2).reshape(
        peer_count * capacity
    )
    arrival_slot = holder * capacity + position
    left_grouped = left_env.reshape(group_count, group_terms, left_count, tile_width, tile_width)
    right_grouped = right_env.reshape(group_count, group_terms, right_count, tile_width, tile_width)

    def apply_terms(sources):
        source_grid = sources.reshape(group_count, left_count, right_count, tile_width, tile_width)
        half_product = jnp.einsum(
            "gtaij,ganjk->gtanik", left_grouped, source_grid, preferred_element_type=jnp.float32
        ).astype(jnp.bfloat16)
        contracted = jnp.einsum(
            "gtanik,gtnkl->anil", half_product, right_grouped, preferred_element_type=jnp.float32
        )
        return contracted.reshape(tile_count, tile_width, tile_width)

    first_arrived = lax.all_to_all(
        psi_first[chosen], "sec", split_axis=0, concat_axis=0, tiled=True
    )
    first_sum = apply_terms(first_arrived[arrival_slot])
    second_arrived = lax.all_to_all(
        psi_second[chosen], "sec", split_axis=0, concat_axis=0, tiled=True
    )
    second_sum = apply_terms(second_arrived[arrival_slot])
    totals = lax.psum((first_sum, second_sum), "op")
    return (totals[0].astype(jnp.bfloat16), totals[1].astype(jnp.bfloat16))


def solution(mesh):
    in_specs = (
        P("sec", None, None),
        P("sec", None, None),
        P("op", "sec", None, None),
        P("op", None, None, None),
        P("op", None),
    )
    out_specs = (P("sec", None, None), P("sec", None, None))
    return jax.shard_map(shards, mesh=mesh, in_specs=in_specs, out_specs=out_specs, check_vma=False)
```

profile of v0, /device:TPU:6, one launch (start us, length us, event | category | flops | bytes accessed | tf_op | source)
XLA Modules:
  0.0 198.6 jit_solution(2086236142596136070)
XLA Ops:
  0.6 0.0 copy-start
  0.7 0.8 compare_reduce_fusion
  1.5 0.7 divide_reduce_fusion
  2.2 0.1 div.55
  2.3 0.1 div.54
  2.4 0.1 ne.124
  2.5 0.1 copy.26
  2.6 0.1 and.93
  2.7 0.1 rem.62
  2.8 0.1 copy.25
  2.9 0.1 copy.29
  3.0 0.1 copy.27
  3.1 0.1 convert_reduce_fusion
  3.3 3.1 %gather_fusion.2 = bf16[64,128,128]{2,1,0:T(8,128)(2,1)} fusion(bf16[12,128,128]{2,1,0:T(8,128)(2,1)} %param.6, s32[1024]{0:T(1024)S(1)} %pad_clamp_fusion.1), kind=kCustom, calls=%fused_computation.2 | custom fusion | bytes 4194560 | tf_op jit(solution)/shard_map/gather | solution.py:59
  6.4 0.0 copy-start.1
  6.4 10.9 %all-to-all-start.1 = ((bf16[64,128,128]{2,1,0:T(8,128)(2,1)}), bf16[64,128,128]{2,1,0:T(8,128)(2,1)S(1)}, u32[]{:S(2)}, u32[]{:S(2)}) async-start(bf16[64,128,128]{2,1,0:T(8,128)(2,1)} %gather_fusion.2), calls=%async_computation.1 | async-start | bytes 4194304 | tf_op jit(solution)/shard_map/all_to_all | solution.py:58
  17.3 0.0 copy-done.1
  17.3 2.2 %gather_fusion = bf16[64,128,128]{2,1,0:T(8,128)(2,1)} fusion(bf16[12,128,128]{2,1,0:T(8,128)(2,1)S(1)} %copy-done.1, s32[1024]{0:T(1024)S(1)} %pad_clamp_fusion.1), kind=kCustom, calls=%fused_computation | custom fusion | bytes 4194560 | tf_op jit(solution)/shard_map/gather | solution.py:55
  19.5 46.8 %all-to-all-done.1 = bf16[64,128,128]{2,1,0:T(8,128)(2,1)S(1)} async-done(((bf16[64,128,128]{2,1,0:T(8,128)(2,1)}), bf16[64,128,128]{2,1,0:T(8,128)(2,1)S(1)}, u32[]{:S(2)}, u32[]{:S(2)}) %all-to-all-start.1) | async-done | bytes 2097184 | tf_op jit(solution)/shard_map/all_to_all | solution.py:58
  66.3 8.3 %all-to-all-start = ((bf16[64,128,128]{2,1,0:T(8,128)(2,1)}), bf16[64,128,128]{2,1,0:T(8,128)(2,1)}, u32[]{:S(2)}, u32[]{:S(2)}) async-start(bf16[64,128,128]{2,1,0:T(8,128)(2,1)} %gather_fusion), calls=%async_computation | async-start | bytes 4194304 | tf_op jit(solution)/shard_map/all_to_all | solution.py:54
  74.6 0.8 bitcast_select_fusion
  75.4 0.2 convert_reduce_fusion.1
  75.6 0.6 gather_fusion.3
  76.2 1.7 convert_bitcast_fusion
  77.9 0.0 copy-done
  77.9 0.8 fusion.7
  78.7 0.0 copy-start.2
  78.7 0.1 copy.43
  78.8 44.6 %all-to-all-done = bf16[64,128,128]{2,1,0:T(8,128)(2,1)} async-done(((bf16[64,128,128]{2,1,0:T(8,128)(2,1)}), bf16[64,128,128]{2,1,0:T(8,128)(2,1)}, u32[]{:S(2)}, u32[]{:S(2)}) %all-to-all-start) | async-done | bytes 2097184 | tf_op jit(solution)/shard_map/all_to_all | solution.py:54
  123.4 2.2 %gather_fusion.1 = bf16[12,128,128]{2,1,0:T(8,128)(2,1)S(1)} fusion(bf16[64,128,128]{2,1,0:T(8,128)(2,1)} %all-to-all-done, s32[1024]{0:T(1024)S(1)} %pad_clamp_fusion), kind=kCustom, calls=%fused_computation.1 | custom fusion | bytes 786480 | tf_op jit(solution)/shard_map/gather | solution.py:57
  125.6 0.0 copy-done.2
  125.7 0.7 convert_bitcast_fusion.1
  126.4 0.8 fusion.4
  127.2 0.1 copy.38
  127.3 71.3 %all-reduce.2 = (bf16[12,128,128]{2,1,0:T(8,128)(2,1)}, bf16[12,128,128]{2,1,0:T(8,128)(2,1)}) all-reduce(f32[12,128,128]{2,1,0:T(8,128)S(1)} %bitcast.81, f32[12,128,128]{2,1,0:T(8,128)S(1)} %bitcast.80), channel_id=1, replica_groups=mesh['op'=8,'sec'=64] {'op'}, use_global_device_ids=true, to_apply=%region_3.4 | all-reduce | flops 393216 | bytes 2359296 | tf_op jit(solution)/shard_map/psum | solution.py:62
  (8 shorter events, 0.1 us)
Async XLA Ops:
  0.6 77.3 %copy-start = (bf16[5,6,128,128]{3,2,1,0:T(8,128)(2,1)S(1)}, bf16[5,6,128,128]{3,2,1,0:T(8,128)(2,1)}, u32[]{:S(2)}) copy-start(bf16[5,6,128,128]{3,2,1,0:T(8,128)(2,1)} %param.8) | copy-start | bytes 2949124
  6.4 10.9 %copy-start.1 = (bf16[12,128,128]{2,1,0:T(8,128)(2,1)S(1)}, bf16[12,128,128]{2,1,0:T(8,128)(2,1)}, u32[]{:S(2)}) copy-start(bf16[12,128,128]{2,1,0:T(8,128)(2,1)} %param.5) | copy-start | bytes 1179652
  6.4 59.9 %all-to-all-start.1 = ((bf16[64,128,128]{2,1,0:T(8,128)(2,1)}), bf16[64,128,128]{2,1,0:T(8,128)(2,1)S(1)}, u32[]{:S(2)}, u32[]{:S(2)}) async-start(bf16[64,128,128]{2,1,0:T(8,128)(2,1)} %gather_fusion.2), calls=%async_computation.1 | async-start | bytes 4194304 | tf_op jit(solution)/shard_map/all_to_all | solution.py:58
  66.3 57.2 %all-to-all-start = ((bf16[64,128,128]{2,1,0:T(8,128)(2,1)}), bf16[64,128,128]{2,1,0:T(8,128)(2,1)}, u32[]{:S(2)}, u32[]{:S(2)}) async-start(bf16[64,128,128]{2,1,0:T(8,128)(2,1)} %gather_fusion), calls=%async_computation | async-start | bytes 4194304 | tf_op jit(solution)/shard_map/all_to_all | solution.py:54
  78.7 46.9 %copy-start.2 = (bf16[5,2,128,128]{3,2,1,0:T(8,128)(2,1)S(1)}, bf16[5,2,128,128]{3,2,1,0:T(8,128)(2,1)}, u32[]{:S(2)}) copy-start(bf16[5,2,128,128]{3,2,1,0:T(8,128)(2,1)} %param.7) | copy-start | bytes 983044
where the time goes:
time: 200 us; the launch traced here: 199 us
  waiting for transfers between devices  91.4 us (46%)
  blocking collectives  71.3 us (36%)
  starting transfers between devices  19.2 us (10%)
  local copies, waits for them, and re-layouts  9.06 us (5%)
  matrix products  4.02 us (2%)
  other arithmetic  2.69 us (1%)
    psum x1, blocking collectives, shards(): totals = lax.psum((first_sum, second_sum), 'op')  71.3 us
    all_to_all x1, waiting for transfers between devices, shards(): lax.all_to_all(psi_second[chosen], 'sec', split_axis=0, concat_axis=0, ti...  46.8 us
    all_to_all x1, waiting for transfers between devices, shards(): lax.all_to_all(psi_first[chosen], 'sec', split_axis=0, concat_axis=0, til...  44.6 us
    all_to_all x1, starting transfers between devices, shards(): lax.all_to_all(psi_second[chosen], 'sec', split_axis=0, concat_axis=0, ti...  10.9 us
    all_to_all x1, starting transfers between devices, shards(): lax.all_to_all(psi_first[chosen], 'sec', split_axis=0, concat_axis=0, til...  8.31 us
  transfers between devices with their start and end apart: 2, of which 2 were waited for; matrix products, arithmetic and copies ran while one was open for 3% of the time, Pallas kernels for 0%

commit v1 on v0

v1 whole, which is shorter than its diff:
```python
import jax
import jax.numpy as jnp
import numpy as np
from jax import lax
from jax.experimental import pallas as pl
from jax.experimental.pallas import tpu as pltpu
from jax.sharding import Mesh, PartitionSpec as P

VMEM_LIMIT = 40 * 1024 * 1024
SLAB = 16


def dot(a, b):
    return jnp.dot(a, b, preferred_element_type=jnp.float32)


def swap_order(outer, inner):
    count = outer * inner
    matrix = np.zeros((count, count), np.float32)
    for o in range(outer):
        for i in range(inner):
            matrix[i * outer + o, o * inner + i] = 1
    return jnp.asarray(matrix, jnp.bfloat16)


def pick_parity(count):
    matrix = np.zeros((2, count, 2 * count), np.float32)
    for r in range(count):
        matrix[0, r, 2 * r] = 1
        matrix[1, r, 2 * r + 1] = 1
    return jnp.asarray(matrix, jnp.bfloat16)


def cut_kernel(which_ref, first_ref, second_ref, order_ref, out_ref):
    tiles, width, _ = first_ref.shape
    half = width // 2
    second = which_ref[0] == 1
    rows = 2 * tiles * SLAB
    for slab in range(half // SLAB):
        parts = []
        for k in range(tiles):
            for top in range(2):
                cut = slice(top * half + slab * SLAB, top * half + (slab + 1) * SLAB)
                parts.append(jnp.where(second, second_ref[k, cut, :], first_ref[k, cut, :]))
        block = dot(order_ref[...], jnp.concatenate(parts, axis=0))
        out_ref[slab * rows : (slab + 1) * rows, :] = block.astype(jnp.bfloat16)


def choose_kernel(pieces_ref, hot_ref, parity_ref, out_ref, wide):
    count = parity_ref.shape[1]
    lanes = pieces_ref.shape[1]
    for b in range(pieces_ref.shape[0] // (2 * count)):
        block = pieces_ref[2 * count * b : 2 * count * (b + 1), :]
        for top in range(2):
            picked = dot(parity_ref[top], block).astype(jnp.bfloat16)
            wide[count * b : count * (b + 1), top * lanes : (top + 1) * lanes] = picked
    step = 256
    for m in range(hot_ref.shape[0] // step):
        out_ref[m * step : (m + 1) * step, :] = dot(
            hot_ref[m * step : (m + 1) * step, :], wide[...]
        ).astype(jnp.bfloat16)


def apply_kernel(arrived_ref, left_a, left_b, right_a, right_b, order_ref, out_ref, tiles, halves):
    terms, lefts, width, _ = left_a.shape
    rights = right_a.shape[1]
    half = width // 2
    units = 2 * lefts * rights
    rows = units * SLAB
    for slab in range(half // SLAB):
        block = dot(order_ref[...], arrived_ref[slab * rows : (slab + 1) * rows, :])
        block = block.astype(jnp.bfloat16)
        for u in range(units):
            g, a, r = u // (lefts * rights), u // rights % lefts, u % rights
            for top in range(2):
                tiles[
                    g,
                    a,
                    top * half + slab * SLAB : top * half + (slab + 1) * SLAB,
                    r * width : (r + 1) * width,
                ] = block[u * SLAB : (u + 1) * SLAB, top * width : (top + 1) * width]
    for g, left in enumerate((left_a, left_b)):
        for a in range(lefts):
            stacked = jnp.concatenate([left[t, a] for t in range(terms)], axis=0)
            product = dot(stacked, tiles[g, a]).astype(jnp.bfloat16)
            for t in range(terms):
                for r in range(rights):
                    column = (g * terms + t) * width
                    halves[r, a * width : (a + 1) * width, column : column + width] = product[
                        t * width : (t + 1) * width, r * width : (r + 1) * width
                    ]
    for r in range(rights):
        stacked = jnp.concatenate(
            [right[t, r] for right in (right_a, right_b) for t in range(terms)], axis=0
        )
        total = dot(halves[r], stacked).astype(jnp.bfloat16)
        for a in range(lefts):
            out_ref[a * rights + r] = total[a * width : (a + 1) * width]


def call(kernel, shape, scratch=(), prefetch=0, name=None, operands=(), flops=0):
    vmem = pl.BlockSpec(memory_space=pltpu.VMEM)
    smem = pl.BlockSpec(memory_space=pltpu.SMEM)
    return pl.pallas_call(
        kernel,
        out_shape=jax.ShapeDtypeStruct(shape, jnp.bfloat16),
        in_specs=[smem] * prefetch + [vmem] * (len(operands) - prefetch),
        out_specs=vmem,
        scratch_shapes=list(scratch),
        compiler_params=pltpu.CompilerParams(vmem_limit_bytes=VMEM_LIMIT),
        cost_estimate=pl.CostEstimate(
            flops=flops, bytes_accessed=4 * 1024 * 1024, transcendentals=0
        ),
        name=name,
    )(*operands)


def shards(psi_first, psi_second, left_env, right_env, links):
    tiles, width, _ = psi_first.shape
    terms, lefts, _, _ = left_env.shape
    rights = right_env.shape[1]
    peers = lax.axis_size("sec")
    every = peers * tiles
    vector = lax.axis_index("v")
    swap = [(0, 1), (1, 0)]

    other_links = lax.ppermute(links, "v", swap)
    pieces = call(
        cut_kernel,
        (peers * 2 * tiles, width),
        prefetch=1,
        name="cut",
        operands=(
            vector.reshape(1).astype(jnp.int32),
            psi_first,
            psi_second,
            swap_order(2 * tiles, SLAB),
        ),
        flops=400_000_000,
    )
    pieces = lax.all_to_all(pieces, "sec", split_axis=0, concat_axis=0, tiled=True)
    other_left = lax.ppermute(left_env, "v", swap)
    other_right = lax.ppermute(right_env, "v", swap)
    wanted = jnp.stack([links.reshape(peers, tiles), other_links.reshape(peers, tiles)], axis=1)
    hot = (wanted.reshape(2 * every, 1) == jnp.arange(every)[None, :]).astype(jnp.bfloat16)
    chosen = call(
        choose_kernel,
        (2 * every, 2 * width),
        scratch=[pltpu.VMEM((every, 2 * width), jnp.bfloat16)],
        name="choose",
        operands=(pieces, hot, pick_parity(8 * tiles)),
        flops=700_000_000,
    )
    arrived = lax.all_to_all(chosen, "sec", split_axis=0, concat_axis=0, tiled=True)
    partial = call(
        apply_kernel,
        (tiles, width, width),
        scratch=[
            pltpu.VMEM((2, lefts, width, rights * width), jnp.bfloat16),
            pltpu.VMEM((rights, lefts * width, 2 * terms * width), jnp.bfloat16),
        ],
        name="apply",
        operands=(
            arrived,
            left_env,
            other_left,
            right_env,
            other_right,
            swap_order(SLAB, 2 * tiles),
        ),
        flops=2_000_000_000,
    )
    quarters = lax.axis_size("q")
    parts = lax.all_to_all(partial, "q", split_axis=0, concat_axis=0, tiled=True)
    parts = parts.reshape(quarters, tiles // quarters, width, width)
    mine = jnp.sum(parts.astype(jnp.float32), axis=0).astype(jnp.bfloat16)
    whole = lax.all_gather(mine, ("q", "v"), axis=0, tiled=False)
    whole = whole.reshape(quarters, 2, tiles // quarters, width, width)
    return (
        whole[:, 0].reshape(tiles, width, width),
        whole[:, 1].reshape(tiles, width, width),
    )


def solution(mesh):
    ops, secs = mesh.devices.shape
    grid = Mesh(mesh.devices.reshape(ops // 2, 2, secs), ("q", "v", "sec"))
    op = ("q", "v")
    in_specs = (
        P("sec", None, None),
        P("sec", None, None),
        P(op, "sec", None, None),
        P(op, None, None, None),
        P(op, None),
    )
    out_specs = (P("sec", None, None), P("sec", None, None))
    return jax.shard_map(shards, mesh=grid, in_specs=in_specs, out_specs=out_specs, check_vma=False)
```

time: 200 us -> 127 us (0.64)
  waiting for transfers between devices: 91.4 us -> 35.6 us
  blocking collectives: 71.3 us -> 49.6 us
  starting transfers between devices: 19.2 us -> 28 us
  Pallas kernels: 0 us -> 5.83 us
  matrix products: 4.02 us -> 0 us
  local copies, waits for them, and re-layouts: 9.06 us -> 5.48 us
    all_to_all x2, waiting for transfers between devices: 91.4 us -> 7.29 us  [the longest x1 7.29 us: shards(): lax.all_to_all(pieces, 'sec', split_axis=0, concat_axis=0, tiled=True)]
    psum x1 -> x0, blocking collectives: 71.3 us -> none  [shards(): totals = lax.psum((first_sum, second_sum), 'op')]
    ppermute x0 -> x3, waiting for transfers between devices: none -> 28.3 us  [the longest x1 27.3 us: shards(): other_left = lax.ppermute(left_env, 'v', swap)]
    all_gather x0 -> x1, blocking collectives: none -> 26.3 us  [shards(): whole = lax.all_gather(mine, ('q', 'v'), axis=0, tiled=False)]
    all_to_all x0 -> x1, blocking collectives: none -> 23.3 us  [shards(): lax.all_to_all(partial, 'q', split_axis=0, concat_axis=0, tiled=True)]
    ppermute x0 -> x3, starting transfers between devices: none -> 10.5 us  [the longest x1 4.29 us: shards(): other_right = lax.ppermute(right_env, 'v', swap)]
    gather x4 -> x0, local copies, waits for them, and re-layouts: 8.11 us -> none  [the longest x1 3.11 us: shards(): psi_second[chosen]]
    pallas_call x0 -> x3, Pallas kernels: none -> 5.83 us  [call(): pl.pallas_call(kernel, out_shape=jax.ShapeDtypeStruct(shape, jnp.bfloat16...]
  transfers between devices with their start and end apart: 2 -> 5, of which waited for: 2 -> 3; matrix products, arithmetic and copies ran while one was open for 3% -> 1% of each run, Pallas kernels for 0% -> 0%
where the time goes in v1:
time: 127 us; the launch traced here: 126 us
  blocking collectives  49.6 us (39%)
  waiting for transfers between devices  35.6 us (28%)
  starting transfers between devices  28 us (22%)
  Pallas kernels  5.83 us (5%)
  local copies, waits for them, and re-layouts  5.48 us (4%)
    ppermute x1, waiting for transfers between devices, shards(): other_left = lax.ppermute(left_env, 'v', swap)  27.3 us
    all_gather x1, blocking collectives, shards(): whole = lax.all_gather(mine, ('q', 'v'), axis=0, tiled=False)  26.3 us
    all_to_all x1, blocking collectives, shards(): lax.all_to_all(partial, 'q', split_axis=0, concat_axis=0, tiled=True)  23.3 us
    all_to_all x1, starting transfers between devices, shards(): lax.all_to_all(pieces, 'sec', split_axis=0, concat_axis=0, tiled=True)  10.8 us
    all_to_all x1, waiting for transfers between devices, shards(): lax.all_to_all(pieces, 'sec', split_axis=0, concat_axis=0, tiled=True)  7.29 us
    all_to_all x1, starting transfers between devices, shards(): lax.all_to_all(chosen, 'sec', split_axis=0, concat_axis=0, tiled=True)  6.67 us
    pallas_call x3, Pallas kernels, call(): pl.pallas_call(kernel, out_shape=jax.ShapeDtypeStruct(shape, jnp.bfloat16...  5.83 us
    ppermute x1, starting transfers between devices, shards(): other_right = lax.ppermute(right_env, 'v', swap)  4.29 us
  transfers between devices with their start and end apart: 5, of which 3 were waited for; matrix products, arithmetic and copies ran while one was open for 1% of the time, Pallas kernels for 0%

profile of v1, /device:TPU:6, one launch (start us, length us, event | category | flops | bytes accessed | tf_op | source)
XLA Modules:
  0.0 126.5 jit_solution(1362711537692710702)
XLA Ops:
  0.6 0.0 copy-start.2
  0.6 1.0 copy-done.2
  1.6 0.0 copy-start.3
  1.6 1.0 copy-done.3
  2.6 0.0 copy-start.6
  2.6 1.0 copy-done.6
  3.6 0.0 copy-start
  3.6 1.2 cut.1
  4.8 10.8 %all-to-all-start = ((bf16[64,24,128]{2,1,0:T(8,128)(2,1)}), bf16[64,24,128]{2,1,0:T(8,128)(2,1)S(1)}, u32[]{:S(2)}, u32[]{:S(2)}) async-start(bf16[64,24,128]{2,1,0:T(8,128)(2,1)} %bitcast.1), calls=%async_computation | async-start | bytes 786432 | tf_op jit(solution)/shard_map/all_to_all | solution.py:141
  15.6 4.3 %collective-permute-start = (s32[1,768]{1,0:T(1,128)}, s32[1,768]{1,0:T(1,128)S(1)}, u32[]{:S(2)}, u32[]{:S(2)}) collective-permute-start(s32[1,768]{1,0:T(1,128)} %param.12), channel_id=1, source_target_pairs={{0,64},{64,0},{1,65},{65,1},{2,66},{66,2},{3,67},{67,3},{4,68},{68... | collective-permute-start | bytes 9224 | tf_op jit(solution)/shard_map/ppermute | solution.py:127
  19.9 0.7 reduce.1
  20.6 0.1 stack_reshape.6
  20.7 1.0 collective-permute-done
  21.7 0.1 stack_reshape.7
  21.8 0.1 copy.14
  21.9 0.1 eq.15
  22.0 0.5 fusion.hot_ref
  22.5 7.3 %all-to-all-done = bf16[64,24,128]{2,1,0:T(8,128)(2,1)S(1)} async-done(((bf16[64,24,128]{2,1,0:T(8,128)(2,1)}), bf16[64,24,128]{2,1,0:T(8,128)(2,1)S(1)}, u32[]{:S(2)}, u32[]{:S(2)}) %all-to-all-start) | async-done | bytes 393248 | tf_op jit(solution)/shard_map/all_to_all | solution.py:141
  29.8 0.0 copy-done
  29.8 0.0 copy-start.4
  29.8 0.0 copy-start.5
  29.8 1.9 %choose.1 = bf16[1536,256]{1,0:T(8,128)(2,1)} custom-call(bf16[1536,128]{1,0:T(8,128)(2,1)S(1)} %bitcast.9, bf16[1536,768]{1,0:T(8,128)(2,1)S(1)} %fusion.hot_ref, bf16[2,96,192]{2,1,0:T(8,128)(2,1)S(1)} %copy-done), custom_call_target="tpu_custom_call" | custom-call | flops 700000000 | bytes 4194304 | tf_op jit(solution)/shard_map/choose/pallas_call | solution.py:104
  31.7 6.7 %all-to-all-start.1 = ((bf16[64,24,256]{2,1,0:T(8,128)(2,1)}), bf16[64,24,256]{2,1,0:T(8,128)(2,1)S(1)}, u32[]{:S(2)}, u32[]{:S(2)}) async-start(bf16[64,24,256]{2,1,0:T(8,128)(2,1)} %bitcast.3), calls=%async_computation.1 | async-start | bytes 1572864 | tf_op jit(solution)/shard_map/all_to_all | solution.py:154
  38.4 4.3 %collective-permute-start.2 = (bf16[5,6,128,128]{3,2,1,0:T(8,128)(2,1)}, bf16[5,6,128,128]{3,2,1,0:T(8,128)(2,1)S(1)}, u32[]{:S(2)}, u32[]{:S(2)}) collective-permute-start(bf16[5,6,128,128]{3,2,1,0:T(8,128)(2,1)} %right_a.1), channel_id=1, source_target_pairs={{0,64},{64,0},{1,65},{65,1},{2,66},{66,2},{3,67},{67,3},{4,68},{68... | collective-permute-start | bytes 2949128 | tf_op jit(solution)/shard_map/ppermute | solution.py:143
  42.7 0.0 copy-done.4
  42.7 1.9 %collective-permute-start.1 = (bf16[5,2,128,128]{3,2,1,0:T(8,128)(2,1)S(1)}, bf16[5,2,128,128]{3,2,1,0:T(8,128)(2,1)S(1)}, u32[]{:S(2)}, u32[]{:S(2)}) collective-permute-start(bf16[5,2,128,128]{3,2,1,0:T(8,128)(2,1)S(1)} %copy-done.4), channel_id=1, source_target_pairs={{0,64},{64,0},{1,65},{65,1},{2,66},{66,2},{3,67},{67,3},{4,68},{68... | collective-permute-start | bytes 983048 | tf_op jit(solution)/shard_map/ppermute | solution.py:142
  44.6 27.3 %collective-permute-done.1.left_b = bf16[5,2,128,128]{3,2,1,0:T(8,128)(2,1)S(1)} collective-permute-done((bf16[5,2,128,128]{3,2,1,0:T(8,128)(2,1)S(1)}, bf16[5,2,128,128]{3,2,1,0:T(8,128)(2,1)S(1)}, u32[]{:S(2)}, u32[]{:S(2)}) %collective-permute-start.1) | collective-permute-done | bytes 327712 | tf_op jit(solution)/shard_map/ppermute | solution.py:142
  71.9 0.0 collective-permute-done.2.right_b
  71.9 0.0 all-to-all-done.1
  71.9 0.0 copy-done.5
  72.0 0.0 copy-start.1
  72.0 1.2 copy-done.1
  73.2 2.7 %apply.1 = bf16[12,128,128]{2,1,0:T(8,128)(2,1)S(1)} custom-call(bf16[1536,256]{1,0:T(8,128)(2,1)S(1)} %bitcast.10, bf16[5,2,128,128]{3,2,1,0:T(8,128)(2,1)S(1)} %copy-done.4, bf16[5,2,128,128]{3,2,1,0:T(8,128)(2,1)S(1)} %collective-permute-done.1.left_b, bf16[5,6,128,128]{3,2,1,0:T(8,128)(2,1)S(1)} %copy-done.1, ...), custom_call_target="tpu_custom_call" | custom-call | flops 2000000000 | bytes 4194304 | tf_op jit(solution)/shard_map/apply/pallas_call | solution.py:104
  75.9 23.3 %all_to_all.27 = bf16[12,128,128]{2,1,0:T(8,128)(2,1)S(1)} all-to-all(bf16[12,128,128]{2,1,0:T(8,128)(2,1)S(1)} %apply.1), channel_id=1, replica_groups=mesh['q'=4,'v'=2,'sec'=64] {'q'}, dimensions={0} | all-to-all | bytes 786432 | tf_op jit(solution)/shard_map/all_to_all | solution.py:174
  99.1 0.1 reduce_sum.12
  99.2 26.3 %all-gather = bf16[24,128,128]{2,1,0:T(8,128)(2,1)S(1)} all-gather(bf16[3,128,128]{2,1,0:T(8,128)(2,1)S(1)} %reduce_sum.12), channel_id=2, replica_groups=mesh['q'=4,'v'=2,'sec'=64] {'q','v'}, dimensions={0}, use_global_device_ids=true | all-gather | bytes 884736 | tf_op jit(solution)/shard_map/all_gather | solution.py:177
  125.5 1.0 fusion.1
  (2 shorter events, 0.0 us)
Async XLA Ops:
  0.6 1.0 copy-start.2
  1.6 1.0 copy-start.3
  2.6 1.0 copy-start.6
  3.6 26.2 %copy-start = (bf16[2,96,192]{2,1,0:T(8,128)(2,1)S(1)}, bf16[2,96,192]{2,1,0:T(8,128)(2,1)}, u32[]{:S(2)}) copy-start(bf16[2,96,192]{2,1,0:T(8,128)(2,1)} %constant.16.clone.parity_ref) | copy-start | bytes 221188
  4.8 25.0 %all-to-all-start = ((bf16[64,24,128]{2,1,0:T(8,128)(2,1)}), bf16[64,24,128]{2,1,0:T(8,128)(2,1)S(1)}, u32[]{:S(2)}, u32[]{:S(2)}) async-start(bf16[64,24,128]{2,1,0:T(8,128)(2,1)} %bitcast.1), calls=%async_computation | async-start | bytes 786432 | tf_op jit(solution)/shard_map/all_to_all | solution.py:141
  15.6 6.1 %collective-permute-start = (s32[1,768]{1,0:T(1,128)}, s32[1,768]{1,0:T(1,128)S(1)}, u32[]{:S(2)}, u32[]{:S(2)}) collective-permute-start(s32[1,768]{1,0:T(1,128)} %param.12), channel_id=1, source_target_pairs={{0,64},{64,0},{1,65},{65,1},{2,66},{66,2},{3,67},{67,3},{4,68},{68... | collective-permute-start | bytes 9224 | tf_op jit(solution)/shard_map/ppermute | solution.py:127
  29.8 12.9 %copy-start.4 = (bf16[5,2,128,128]{3,2,1,0:T(8,128)(2,1)S(1)}, bf16[5,2,128,128]{3,2,1,0:T(8,128)(2,1)}, u32[]{:S(2)}) copy-start(bf16[5,2,128,128]{3,2,1,0:T(8,128)(2,1)} %left_a.1) | copy-start | bytes 983044
  29.8 42.2 %copy-start.5 = (bf16[384,384]{1,0:T(8,128)(2,1)S(1)}, bf16[384,384]{1,0:T(8,128)(2,1)}, u32[]{:S(2)}) copy-start(bf16[384,384]{1,0:T(8,128)(2,1)} %constant.17.clone.order_ref) | copy-start | bytes 884740
  31.7 40.3 %all-to-all-start.1 = ((bf16[64,24,256]{2,1,0:T(8,128)(2,1)}), bf16[64,24,256]{2,1,0:T(8,128)(2,1)S(1)}, u32[]{:S(2)}, u32[]{:S(2)}) async-start(bf16[64,24,256]{2,1,0:T(8,128)(2,1)} %bitcast.3), calls=%async_computation.1 | async-start | bytes 1572864 | tf_op jit(solution)/shard_map/all_to_all | solution.py:154
  38.4 33.6 %collective-permute-start.2 = (bf16[5,6,128,128]{3,2,1,0:T(8,128)(2,1)}, bf16[5,6,128,128]{3,2,1,0:T(8,128)(2,1)S(1)}, u32[]{:S(2)}, u32[]{:S(2)}) collective-permute-start(bf16[5,6,128,128]{3,2,1,0:T(8,128)(2,1)} %right_a.1), channel_id=1, source_target_pairs={{0,64},{64,0},{1,65},{65,1},{2,66},{66,2},{3,67},{67,3},{4,68},{68... | collective-permute-start | bytes 2949128 | tf_op jit(solution)/shard_map/ppermute | solution.py:143
  42.7 29.3 %collective-permute-start.1 = (bf16[5,2,128,128]{3,2,1,0:T(8,128)(2,1)S(1)}, bf16[5,2,128,128]{3,2,1,0:T(8,128)(2,1)S(1)}, u32[]{:S(2)}, u32[]{:S(2)}) collective-permute-start(bf16[5,2,128,128]{3,2,1,0:T(8,128)(2,1)S(1)} %copy-done.4), channel_id=1, source_target_pairs={{0,64},{64,0},{1,65},{65,1},{2,66},{66,2},{3,67},{67,3},{4,68},{68... | collective-permute-start | bytes 983048 | tf_op jit(solution)/shard_map/ppermute | solution.py:142
  72.0 1.2 copy-start.1

commit v2 on v1

--- a/solution.py
+++ b/solution.py
@@ -6,8 +6,11 @@
 from jax.experimental.pallas import tpu as pltpu
 from jax.sharding import Mesh, PartitionSpec as P
 
-VMEM_LIMIT = 40 * 1024 * 1024
+VMEM_LIMIT = 30 * 1024 * 1024
+VMEM_WHOLE = 60 * 1024 * 1024
 SLAB = 16
+CHUNKS = 4
+SEC = ("chip", "core")
 
 
 def dot(a, b):
@@ -31,18 +34,36 @@
     return jnp.asarray(matrix, jnp.bfloat16)
 
 
-def cut_kernel(which_ref, first_ref, second_ref, order_ref, out_ref):
+def cut_kernel(first_ref, second_ref, order_ref, out_ref, held, order, sems):
     tiles, width, _ = first_ref.shape
     half = width // 2
-    second = which_ref[0] == 1
+    vector = lax.axis_index("v")
+    order_copy = pltpu.make_async_copy(order_ref, order, sems.at[0])
+
+    def fetch(source, chunk):
+        count = tiles // CHUNKS
+        span = pl.ds(chunk * count, count)
+        return pltpu.make_async_copy(source.at[span], held.at[span], sems.at[1 + chunk])
+
+    order_copy.start()
+    for number, source in enumerate((first_ref, second_ref)):
+
+        @pl.when(vector == number)
+        def _():
+            for chunk in range(CHUNKS):
+                fetch(source, chunk).start()
+
+    order_copy.wait()
+    for chunk in range(CHUNKS):
+        fetch(first_ref, chunk).wait()
     rows = 2 * tiles * SLAB
     for slab in range(half // SLAB):
         parts = []
         for k in range(tiles):
             for top in range(2):
-                cut = slice(top * half + slab * SLAB, top * half + (slab + 1) * SLAB)
-                parts.append(jnp.where(second, second_ref[k, cut, :], first_ref[k, cut, :]))
-        block = dot(order_ref[...], jnp.concatenate(parts, axis=0))
+                start = top * half + slab * SLAB
+                parts.append(held[k, start : start + SLAB, :])
+        block = dot(order[...], jnp.concatenate(parts, axis=0))
         out_ref[slab * rows : (slab + 1) * rows, :] = block.astype(jnp.bfloat16)
 
 
@@ -61,12 +82,25 @@
         ).astype(jnp.bfloat16)
 
 
-def apply_kernel(arrived_ref, left_a, left_b, right_a, right_b, order_ref, out_ref, tiles, halves):
+def apply_kernel(
+    arrived_ref,
+    left_a,
+    left_b,
+    right_a,
+    near_ref,
+    far_ref,
+    order_ref,
+    out_ref,
+    tiles,
+    halves,
+):
     terms, lefts, width, _ = left_a.shape
     rights = right_a.shape[1]
+    upper = near_ref.shape[1]
     half = width // 2
     units = 2 * lefts * rights
     rows = units * SLAB
+    second = lax.axis_index("core") == 1
     for slab in range(half // SLAB):
         block = dot(order_ref[...], arrived_ref[slab * rows : (slab + 1) * rows, :])
         block = block.astype(jnp.bfloat16)
@@ -90,24 +124,29 @@
                         t * width : (t + 1) * width, r * width : (r + 1) * width
                     ]
     for r in range(rights):
+        side = 0 if r < upper else 1
+        place = r - side * (rights - upper)
+        mine, other = (near_ref, far_ref) if side == 0 else (far_ref, near_ref)
         stacked = jnp.concatenate(
-            [right[t, r] for right in (right_a, right_b) for t in range(terms)], axis=0
+            [right_a[t, r] for t in range(terms)]
+            + [jnp.where(second, other[t, place], mine[t, place]) for t in range(terms)],
+            axis=0,
         )
         total = dot(halves[r], stacked).astype(jnp.bfloat16)
         for a in range(lefts):
             out_ref[a * rights + r] = total[a * width : (a + 1) * width]
 
 
-def call(kernel, shape, scratch=(), prefetch=0, name=None, operands=(), flops=0):
+def call(kernel, shape, operands, fetched, scratch=(), name=None, flops=0, limit=VMEM_LIMIT):
     vmem = pl.BlockSpec(memory_space=pltpu.VMEM)
-    smem = pl.BlockSpec(memory_space=pltpu.SMEM)
+    anywhere = pl.BlockSpec(memory_space=pltpu.HBM)
     return pl.pallas_call(
         kernel,
         out_shape=jax.ShapeDtypeStruct(shape, jnp.bfloat16),
-        in_specs=[smem] * prefetch + [vmem] * (len(operands) - prefetch),
+        in_specs=[anywhere] * fetched + [vmem] * (len(operands) - fetched),
         out_specs=vmem,
         scratch_shapes=list(scratch),
-        compiler_params=pltpu.CompilerParams(vmem_limit_bytes=VMEM_LIMIT),
+        compiler_params=pltpu.CompilerParams(vmem_limit_bytes=limit),
         cost_estimate=pl.CostEstimate(
             flops=flops, bytes_accessed=4 * 1024 * 1024, transcendentals=0
         ),
@@ -119,55 +158,58 @@
     tiles, width, _ = psi_first.shape
     terms, lefts, _, _ = left_env.shape
     rights = right_env.shape[1]
-    peers = lax.axis_size("sec")
+    peers = lax.axis_size(SEC)
     every = peers * tiles
-    vector = lax.axis_index("v")
     swap = [(0, 1), (1, 0)]
 
+    slab_rows = 2 * tiles * SLAB
+    order_shape = pltpu.VMEM((slab_rows, slab_rows), jnp.bfloat16)
+
+    upper = (rights + 1) // 2
+    core = lax.axis_index("core")
+    near = lax.dynamic_slice_in_dim(right_env, core * (rights - upper), upper, 1)
+    near = lax.ppermute(near, "v", swap)
+    far = lax.ppermute(near, "core", swap)
     other_links = lax.ppermute(links, "v", swap)
     pieces = call(
         cut_kernel,
         (peers * 2 * tiles, width),
-        prefetch=1,
+        (psi_first, psi_second, swap_order(2 * tiles, SLAB)),
+        3,
+        scratch=[
+            pltpu.VMEM((tiles, width, width), jnp.bfloat16),
+            order_shape,
+            pltpu.SemaphoreType.DMA((1 + CHUNKS,)),
+        ],
         name="cut",
-        operands=(
-            vector.reshape(1).astype(jnp.int32),
-            psi_first,
-            psi_second,
-            swap_order(2 * tiles, SLAB),
-        ),
+        limit=VMEM_WHOLE,
         flops=400_000_000,
     )
-    pieces = lax.all_to_all(pieces, "sec", split_axis=0, concat_axis=0, tiled=True)
+    pieces = lax.all_to_all(pieces, SEC, split_axis=0, concat_axis=0, tiled=True)
     other_left = lax.ppermute(left_env, "v", swap)
-    other_right = lax.ppermute(right_env, "v", swap)
     wanted = jnp.stack([links.reshape(peers, tiles), other_links.reshape(peers, tiles)], axis=1)
     hot = (wanted.reshape(2 * every, 1) == jnp.arange(every)[None, :]).astype(jnp.bfloat16)
     chosen = call(
         choose_kernel,
         (2 * every, 2 * width),
+        (pieces, hot, pick_parity(8 * tiles)),
+        0,
         scratch=[pltpu.VMEM((every, 2 * width), jnp.bfloat16)],
         name="choose",
-        operands=(pieces, hot, pick_parity(8 * tiles)),
         flops=700_000_000,
     )
-    arrived = lax.all_to_all(chosen, "sec", split_axis=0, concat_axis=0, tiled=True)
+    chosen, other_left = lax.optimization_barrier((chosen, other_left))
+    arrived = lax.all_to_all(chosen, SEC, split_axis=0, concat_axis=0, tiled=True)
     partial = call(
         apply_kernel,
         (tiles, width, width),
+        (arrived, left_env, other_left, right_env, near, far, swap_order(SLAB, 2 * tiles)),
+        0,
         scratch=[
             pltpu.VMEM((2, lefts, width, rights * width), jnp.bfloat16),
             pltpu.VMEM((rights, lefts * width, 2 * terms * width), jnp.bfloat16),
         ],
         name="apply",
-        operands=(
-            arrived,
-            left_env,
-            other_left,
-            right_env,
-            other_right,
-            swap_order(SLAB, 2 * tiles),
-        ),
         flops=2_000_000_000,
     )
     quarters = lax.axis_size("q")
@@ -184,14 +226,14 @@
 
 def solution(mesh):
     ops, secs = mesh.devices.shape
-    grid = Mesh(mesh.devices.reshape(ops // 2, 2, secs), ("q", "v", "sec"))
-    op = ("q", "v")
+    grid = Mesh(mesh.devices.reshape(ops // 2, 2, secs // 2, 2), ("q", "v", "chip", "core"))
+    op, sec = ("q", "v"), SEC
     in_specs = (
-        P("sec", None, None),
-        P("sec", None, None),
-        P(op, "sec", None, None),
+        P(sec, None, None),
+        P(sec, None, None),
+        P(op, sec, None, None),
         P(op, None, None, None),
         P(op, None),
     )
-    out_specs = (P("sec", None, None), P("sec", None, None))
+    out_specs = (P(sec, None, None), P(sec, None, None))
     return jax.shard_map(shards, mesh=grid, in_specs=in_specs, out_specs=out_specs, check_vma=False)

time: 127 us -> 117 us (0.921)
  waiting for transfers between devices: 35.6 us -> 23 us
  starting transfers between devices: 28 us -> 31.3 us
  local copies, waits for them, and re-layouts: 5.48 us -> 3.37 us
    ppermute x1, waiting for transfers between devices: 27.3 us -> 0.01 us  [shards(): other_left = lax.ppermute(left_env, 'v', swap)]
    ppermute x1 -> x2, waiting for transfers between devices: 0.01 us -> 14.8 us  [the longest x1 13 us: shards(): near = lax.ppermute(near, 'v', swap)]
    all_to_all x2, starting transfers between devices: 17.5 us -> 21 us  [the longest x1 10.8 us: shards(): lax.all_to_all(pieces, SEC, split_axis=0, concat_axis=0, tiled=True)]
    unnamed x14 -> x8, local copies, waits for them, and re-layouts: 4.15 us -> 0.98 us
    ppermute x1 -> x2, starting transfers between devices: 4.29 us -> 4.11 us  [the longest x1 2.2 us: shards(): near = lax.ppermute(near, 'v', swap)]
  transfers between devices with their start and end apart: 5 -> 6, of which waited for: 3 -> 4; matrix products, arithmetic and copies ran while one was open for 1% -> 2% of each run, Pallas kernels for 0% -> 2%
where the time goes in v2:
time: 117 us
  blocking collectives  49.8 us (43%)
  starting transfers between devices  31.3 us (27%)
  waiting for transfers between devices  23 us (20%)
  Pallas kernels  7.03 us (6%)
  local copies, waits for them, and re-layouts  3.37 us (3%)
  other arithmetic  1.24 us (1%)
    all_gather x1, blocking collectives, shards(): whole = lax.all_gather(mine, ('q', 'v'), axis=0, tiled=False)  26.2 us
    all_to_all x1, blocking collectives, shards(): lax.all_to_all(partial, 'q', split_axis=0, concat_axis=0, tiled=True)  23.6 us
    ppermute x1, waiting for transfers between devices, shards(): near = lax.ppermute(near, 'v', swap)  13 us
    all_to_all x1, starting transfers between devices, shards(): lax.all_to_all(pieces, SEC, split_axis=0, concat_axis=0, tiled=True)  10.8 us
    all_to_all x1, starting transfers between devices, shards(): lax.all_to_all(chosen, SEC, split_axis=0, concat_axis=0, tiled=True)  10.1 us
    pallas_call x3, Pallas kernels, call(): pl.pallas_call(kernel, out_shape=jax.ShapeDtypeStruct(shape, jnp.bfloat16...  7.03 us
    all_to_all x1, waiting for transfers between devices, shards(): lax.all_to_all(pieces, SEC, split_axis=0, concat_axis=0, tiled=True)  6.31 us
    ppermute x1, starting transfers between devices, shards(): other_links = lax.ppermute(links, 'v', swap)  4.28 us
  transfers between devices with their start and end apart: 6, of which 4 were waited for; matrix products, arithmetic and copies ran while one was open for 2% of the time, Pallas kernels for 2%

profile of v2, /device:TPU:6, one launch (start us, length us, event | category | flops | bytes accessed | tf_op | source)
XLA Modules:
  0.0 116.5 jit_solution(3692817185906548736)
XLA Ops:
  0.6 0.0 copy-start.1
  0.6 2.4 %cut.1 = bf16[1536,128]{1,0:T(8,128)(2,1)} custom-call(bf16[12,128,128]{2,1,0:T(8,128)(2,1)} %first_ref.1, bf16[12,128,128]{2,1,0:T(8,128)(2,1)} %second_ref.1, bf16[384,384]{1,0:T(8,128)(2,1)} %constant.19.clone.order_ref), custom_call_target="tpu_custom_call" | custom-call | flops 400000000 | bytes 4194304 | tf_op jit(solution)/shard_map/cut/pallas_call | solution.py:143
  3.1 10.8 %all-to-all-start = ((bf16[64,24,128]{2,1,0:T(8,128)(2,1)}), bf16[64,24,128]{2,1,0:T(8,128)(2,1)S(1)}, u32[]{:S(2)}, u32[]{:S(2)}) async-start(bf16[64,24,128]{2,1,0:T(8,128)(2,1)} %bitcast.12), calls=%async_computation | async-start | bytes 786432 | tf_op jit(solution)/shard_map/all_to_all | solution.py:188
  13.9 4.3 %collective-permute-start = (s32[1,768]{1,0:T(1,128)}, s32[1,768]{1,0:T(1,128)S(1)}, u32[]{:S(2)}, u32[]{:S(2)}) collective-permute-start(s32[1,768]{1,0:T(1,128)} %param.12), channel_id=1, source_target_pairs={{0,64},{64,0},{1,65},{65,1},{2,66},{66,2},{3,67},{67,3},{4,68},{68... | collective-permute-start | bytes 9224 | tf_op jit(solution)/shard_map/ppermute | solution.py:173
  18.2 1.9 %collective-permute-start.1 = (bf16[5,2,128,128]{3,2,1,0:T(8,128)(2,1)}, bf16[5,2,128,128]{3,2,1,0:T(8,128)(2,1)S(1)}, u32[]{:S(2)}, u32[]{:S(2)}) collective-permute-start(bf16[5,2,128,128]{3,2,1,0:T(8,128)(2,1)} %left_a.1), channel_id=1, source_target_pairs={{0,64},{64,0},{1,65},{65,1},{2,66},{66,2},{3,67},{67,3},{4,68},{68... | collective-permute-start | bytes 983048 | tf_op jit(solution)/shard_map/ppermute | solution.py:189
  20.1 0.7 reduce.1
  20.8 0.1 stack_reshape.6
  20.9 0.0 collective-permute-done
  20.9 0.1 stack_reshape.7
  21.1 0.1 copy.14
  21.1 0.1 eq.15
  21.3 0.5 fusion.hot_ref
  21.7 6.3 %all-to-all-done = bf16[64,24,128]{2,1,0:T(8,128)(2,1)S(1)} async-done(((bf16[64,24,128]{2,1,0:T(8,128)(2,1)}), bf16[64,24,128]{2,1,0:T(8,128)(2,1)S(1)}, u32[]{:S(2)}, u32[]{:S(2)}) %all-to-all-start) | async-done | bytes 393248 | tf_op jit(solution)/shard_map/all_to_all | solution.py:188
  28.0 0.0 copy-done.1
  28.0 0.0 copy-start.2
  28.0 1.9 %choose.1 = bf16[1536,256]{1,0:T(8,128)(2,1)} custom-call(bf16[1536,128]{1,0:T(8,128)(2,1)S(1)} %bitcast.8, bf16[1536,768]{1,0:T(8,128)(2,1)S(1)} %fusion.hot_ref, bf16[2,96,192]{2,1,0:T(8,128)(2,1)S(1)} %copy-done.1), custom_call_target="tpu_custom_call" | custom-call | flops 700000000 | bytes 4194304 | tf_op jit(solution)/shard_map/choose/pallas_call | solution.py:143
  29.9 0.0 copy-start
  29.9 0.0 collective-permute-done.1.left_b
  29.9 10.1 %all-to-all-start.1 = ((bf16[64,24,256]{2,1,0:T(8,128)(2,1)}), bf16[64,24,256]{2,1,0:T(8,128)(2,1)S(1)}, u32[]{:S(2)}, u32[]{:S(2)}) async-start(bf16[64,24,256]{2,1,0:T(8,128)(2,1)} %bitcast.2), calls=%async_computation.1 | async-start | bytes 1572864 | tf_op jit(solution)/shard_map/all_to_all | solution.py:202
  40.1 1.1 constant_dynamic-slice_fusion
  41.2 2.2 %collective-permute-start.2 = (bf16[5,3,128,128]{3,2,1,0:T(8,128)(2,1)S(1)}, bf16[5,3,128,128]{3,2,1,0:T(8,128)(2,1)S(1)}, u32[]{:S(2)}, u32[]{:S(2)}) collective-permute-start(bf16[5,3,128,128]{3,2,1,0:T(8,128)(2,1)S(1)} %constant_dynamic-slice_fusion), channel_id=1, source_target_pairs={{0,64},{64,0},{1,65},{65,1},{2,66},{66,2},{3,67},{67,3},{4,68},{68... | collective-permute-start | bytes 1474568 | tf_op jit(solution)/shard_map/ppermute | solution.py:171
  43.4 13.0 %collective-permute-done.2.near_ref = bf16[5,3,128,128]{3,2,1,0:T(8,128)(2,1)S(1)} collective-permute-done((bf16[5,3,128,128]{3,2,1,0:T(8,128)(2,1)S(1)}, bf16[5,3,128,128]{3,2,1,0:T(8,128)(2,1)S(1)}, u32[]{:S(2)}, u32[]{:S(2)}) %collective-permute-start.2) | collective-permute-done | bytes 491552 | tf_op jit(solution)/shard_map/ppermute | solution.py:171
  56.3 1.9 %collective-permute-start.3 = (bf16[5,3,128,128]{3,2,1,0:T(8,128)(2,1)S(1)}, bf16[5,3,128,128]{3,2,1,0:T(8,128)(2,1)S(1)}, u32[]{:S(2)}, u32[]{:S(2)}) collective-permute-start(bf16[5,3,128,128]{3,2,1,0:T(8,128)(2,1)S(1)} %collective-permute-done.2.near_ref), channel_id=1, source_target_pairs={{0,1},{1,0},{2,3},{3,2},{4,5},{5,4},{6,7},{7,6},{8,9},{9,8},{10,11... | collective-permute-start | bytes 1474568 | tf_op jit(solution)/shard_map/ppermute | solution.py:172
  58.3 1.8 %collective-permute-done.3.far_ref = bf16[5,3,128,128]{3,2,1,0:T(8,128)(2,1)S(1)} collective-permute-done((bf16[5,3,128,128]{3,2,1,0:T(8,128)(2,1)S(1)}, bf16[5,3,128,128]{3,2,1,0:T(8,128)(2,1)S(1)}, u32[]{:S(2)}, u32[]{:S(2)}) %collective-permute-start.3) | collective-permute-done | bytes 491552 | tf_op jit(solution)/shard_map/ppermute | solution.py:172
  60.1 1.9 %all-to-all-done.1 = bf16[64,24,256]{2,1,0:T(8,128)(2,1)S(1)} async-done(((bf16[64,24,256]{2,1,0:T(8,128)(2,1)}), bf16[64,24,256]{2,1,0:T(8,128)(2,1)S(1)}, u32[]{:S(2)}, u32[]{:S(2)}) %all-to-all-start.1) | async-done | bytes 786464 | tf_op jit(solution)/shard_map/all_to_all | solution.py:202
  62.0 0.0 copy-done.2
  62.0 0.0 copy-done
  62.0 0.0 copy-start.3
  62.0 1.0 copy-done.3
  63.0 2.7 %apply.1 = bf16[12,128,128]{2,1,0:T(8,128)(2,1)S(1)} custom-call(bf16[1536,256]{1,0:T(8,128)(2,1)S(1)} %bitcast.9, bf16[5,2,128,128]{3,2,1,0:T(8,128)(2,1)S(1)} %copy-done.2, bf16[5,2,128,128]{3,2,1,0:T(8,128)(2,1)S(1)} %collective-permute-done.1.left_b, bf16[5,6,128,128]{3,2,1,0:T(8,128)(2,1)S(1)} %copy-done, ...), custom_call_target="tpu_custom_call" | custom-call | flops 2000000000 | bytes 4194304 | tf_op jit(solution)/shard_map/apply/pallas_call | solution.py:143
  65.7 23.6 %all_to_all.27 = bf16[12,128,128]{2,1,0:T(8,128)(2,1)S(1)} all-to-all(bf16[12,128,128]{2,1,0:T(8,128)(2,1)S(1)} %apply.1), channel_id=1, replica_groups=mesh['q'=4,'v'=2,'chip'=32,'core'=2] {'q'}, dimensions={0} | all-to-all | bytes 786432 | tf_op jit(solution)/shard_map/all_to_all | solution.py:216
  89.3 0.1 reduce_sum.12
  89.4 26.2 %all-gather = bf16[24,128,128]{2,1,0:T(8,128)(2,1)S(1)} all-gather(bf16[3,128,128]{2,1,0:T(8,128)(2,1)S(1)} %reduce_sum.12), channel_id=2, replica_groups=mesh['q'=4,'v'=2,'chip'=32,'core'=2] {'q','v'}, dimensions={0}, use_global_device_ids=true | all-gather | bytes 884736 | tf_op jit(solution)/shard_map/all_gather | solution.py:219
  115.6 1.0 fusion.1
  (2 shorter events, 0.0 us)
Async XLA Ops:
  0.6 27.4 %copy-start.1 = (bf16[2,96,192]{2,1,0:T(8,128)(2,1)S(1)}, bf16[2,96,192]{2,1,0:T(8,128)(2,1)}, u32[]{:S(2)}) copy-start(bf16[2,96,192]{2,1,0:T(8,128)(2,1)} %constant.20.clone.parity_ref) | copy-start | bytes 221188
  3.1 25.0 %all-to-all-start = ((bf16[64,24,128]{2,1,0:T(8,128)(2,1)}), bf16[64,24,128]{2,1,0:T(8,128)(2,1)S(1)}, u32[]{:S(2)}, u32[]{:S(2)}) async-start(bf16[64,24,128]{2,1,0:T(8,128)(2,1)} %bitcast.12), calls=%async_computation | async-start | bytes 786432 | tf_op jit(solution)/shard_map/all_to_all | solution.py:188
  13.9 7.0 %collective-permute-start = (s32[1,768]{1,0:T(1,128)}, s32[1,768]{1,0:T(1,128)S(1)}, u32[]{:S(2)}, u32[]{:S(2)}) collective-permute-start(s32[1,768]{1,0:T(1,128)} %param.12), channel_id=1, source_target_pairs={{0,64},{64,0},{1,65},{65,1},{2,66},{66,2},{3,67},{67,3},{4,68},{68... | collective-permute-start | bytes 9224 | tf_op jit(solution)/shard_map/ppermute | solution.py:173
  18.2 11.8 %collective-permute-start.1 = (bf16[5,2,128,128]{3,2,1,0:T(8,128)(2,1)}, bf16[5,2,128,128]{3,2,1,0:T(8,128)(2,1)S(1)}, u32[]{:S(2)}, u32[]{:S(2)}) collective-permute-start(bf16[5,2,128,128]{3,2,1,0:T(8,128)(2,1)} %left_a.1), channel_id=1, source_target_pairs={{0,64},{64,0},{1,65},{65,1},{2,66},{66,2},{3,67},{67,3},{4,68},{68... | collective-permute-start | bytes 983048 | tf_op jit(solution)/shard_map/ppermute | solution.py:189
  28.0 34.0 %copy-start.2 = (bf16[5,2,128,128]{3,2,1,0:T(8,128)(2,1)S(1)}, bf16[5,2,128,128]{3,2,1,0:T(8,128)(2,1)}, u32[]{:S(2)}) copy-start(bf16[5,2,128,128]{3,2,1,0:T(8,128)(2,1)} %left_a.1) | copy-start | bytes 983044
  29.9 32.1 %copy-start = (bf16[5,6,128,128]{3,2,1,0:T(8,128)(2,1)S(1)}, bf16[5,6,128,128]{3,2,1,0:T(8,128)(2,1)}, u32[]{:S(2)}) copy-start(bf16[5,6,128,128]{3,2,1,0:T(8,128)(2,1)} %right_a.1) | copy-start | bytes 2949124
  29.9 32.1 %all-to-all-start.1 = ((bf16[64,24,256]{2,1,0:T(8,128)(2,1)}), bf16[64,24,256]{2,1,0:T(8,128)(2,1)S(1)}, u32[]{:S(2)}, u32[]{:S(2)}) async-start(bf16[64,24,256]{2,1,0:T(8,128)(2,1)} %bitcast.2), calls=%async_computation.1 | async-start | bytes 1572864 | tf_op jit(solution)/shard_map/all_to_all | solution.py:202
  41.2 15.2 %collective-permute-start.2 = (bf16[5,3,128,128]{3,2,1,0:T(8,128)(2,1)S(1)}, bf16[5,3,128,128]{3,2,1,0:T(8,128)(2,1)S(1)}, u32[]{:S(2)}, u32[]{:S(2)}) collective-permute-start(bf16[5,3,128,128]{3,2,1,0:T(8,128)(2,1)S(1)} %constant_dynamic-slice_fusion), channel_id=1, source_target_pairs={{0,64},{64,0},{1,65},{65,1},{2,66},{66,2},{3,67},{67,3},{4,68},{68... | collective-permute-start | bytes 1474568 | tf_op jit(solution)/shard_map/ppermute | solution.py:171
  56.3 3.7 %collective-permute-start.3 = (bf16[5,3,128,128]{3,2,1,0:T(8,128)(2,1)S(1)}, bf16[5,3,128,128]{3,2,1,0:T(8,128)(2,1)S(1)}, u32[]{:S(2)}, u32[]{:S(2)}) collective-permute-start(bf16[5,3,128,128]{3,2,1,0:T(8,128)(2,1)S(1)} %collective-permute-done.2.near_ref), channel_id=1, source_target_pairs={{0,1},{1,0},{2,3},{3,2},{4,5},{5,4},{6,7},{7,6},{8,9},{9,8},{10,11... | collective-permute-start | bytes 1474568 | tf_op jit(solution)/shard_map/ppermute | solution.py:172
  62.0 1.0 copy-start.3

commit v3 on v2

v3 whole, which is shorter than its diff:
```python
import jax
import jax.numpy as jnp
from jax import lax
from jax.experimental import pallas as pl
from jax.experimental.pallas import tpu as pltpu
from jax.sharding import Mesh, PartitionSpec as P

VMEM_LIMIT = 30 * 1024 * 1024
VMEM_WHOLE = 60 * 1024 * 1024
SLAB = 16
CHUNKS = 4
SEC = ("chip", "core")


def dot(a, b):
    return jnp.dot(a, b, preferred_element_type=jnp.float32)


def ones_where(condition):
    return jnp.where(condition, 1.0, 0.0).astype(jnp.bfloat16)


def iotas(rows, columns):
    shape = (rows, columns)
    return (
        lax.broadcasted_iota(jnp.int32, shape, 0),
        lax.broadcasted_iota(jnp.int32, shape, 1),
    )


def cut_kernel(first_ref, second_ref, out_ref, held, cut, fetch_sems, send_sems):
    tiles, width, _ = first_ref.shape
    half = width // 2
    slabs = half // SLAB
    rows = 2 * tiles * SLAB
    vector = lax.axis_index("v")

    def fetch(source, chunk):
        span = pl.ds(chunk * (tiles // CHUNKS), tiles // CHUNKS)
        return pltpu.make_async_copy(source.at[span], held.at[span], fetch_sems.at[chunk])

    def send(slab):
        return pltpu.make_async_copy(
            cut.at[slab], out_ref.at[pl.ds(slab * rows, rows)], send_sems.at[slab]
        )

    for number, source in enumerate((first_ref, second_ref)):

        @pl.when(vector == number)
        def _():
            for chunk in range(CHUNKS):
                fetch(source, chunk).start()

    unit = lax.broadcasted_iota(jnp.int32, (1, rows), 1)
    place, unit = unit % SLAB, unit // SLAB
    target = place * 2 * tiles + unit % tiles * 2 + unit // tiles
    order = ones_where(lax.broadcasted_iota(jnp.int32, (rows, rows), 0) == target)
    for chunk in range(CHUNKS):
        fetch(first_ref, chunk).wait()
    for slab in range(slabs):
        starts = [top * half + slab * SLAB for top in range(2)]
        block = jnp.concatenate(
            [held[k, start : start + SLAB, :] for start in starts for k in range(tiles)], axis=0
        )
        cut[slab] = dot(order, block).astype(jnp.bfloat16)
        send(slab).start()
    for slab in range(slabs):
        send(slab).wait()


def choose_kernel(pieces_ref, hot_ref, out_ref, wide):
    count = 96
    lanes = pieces_ref.shape[1]
    row, column = iotas(count, 2 * count)
    parity = [ones_where(column == 2 * row + top) for top in range(2)]
    for b in range(pieces_ref.shape[0] // (2 * count)):
        block = pieces_ref[2 * count * b : 2 * count * (b + 1), :]
        for top in range(2):
            picked = dot(parity[top], block).astype(jnp.bfloat16)
            wide[count * b : count * (b + 1), top * lanes : (top + 1) * lanes] = picked
    step = 256
    for m in range(hot_ref.shape[0] // step):
        out_ref[m * step : (m + 1) * step, :] = dot(
            hot_ref[m * step : (m + 1) * step, :], wide[...]
        ).astype(jnp.bfloat16)


def apply_kernel(
    arrived_ref,
    left_a,
    left_b,
    right_a,
    near_ref,
    far_ref,
    out_ref,
    tiles,
    halves,
):
    terms, lefts, width, _ = left_a.shape
    rights = right_a.shape[1]
    upper = near_ref.shape[1]
    half = width // 2
    units = 2 * lefts * rights
    part = SLAB // 2
    rows = units * part
    second = lax.axis_index("core") == 1
    row, column = iotas(rows, rows)
    order = ones_where(column == row % part * units + row // part)
    for slab in range(half // SLAB):
        blocks = [
            dot(order, arrived_ref[(2 * slab + p) * rows : (2 * slab + p + 1) * rows, :])
            for p in range(2)
        ]
        for u in range(units):
            g, a, r = u // (lefts * rights), u // rights % lefts, u % rights
            unit = jnp.concatenate([block[u * part : (u + 1) * part] for block in blocks], axis=0)
            unit = unit.astype(jnp.bfloat16)
            for top in range(2):
                tiles[
                    g,
                    a,
                    top * half + slab * SLAB : top * half + (slab + 1) * SLAB,
                    r * width : (r + 1) * width,
                ] = unit[:, top * width : (top + 1) * width]
    for g, left in enumerate((left_a, left_b)):
        for a in range(lefts):
            stacked = jnp.concatenate([left[t, a] for t in range(terms)], axis=0)
            product = dot(stacked, tiles[g, a]).astype(jnp.bfloat16)
            for t in range(terms):
                for r in range(rights):
                    column = (g * terms + t) * width
                    halves[r, a * width : (a + 1) * width, column : column + width] = product[
                        t * width : (t + 1) * width, r * width : (r + 1) * width
                    ]
    for r in range(rights):
        side = 0 if r < upper else 1
        place = r - side * (rights - upper)
        mine, other = (near_ref, far_ref) if side == 0 else (far_ref, near_ref)
        stacked = jnp.concatenate(
            [right_a[t, r] for t in range(terms)]
            + [jnp.where(second, other[t, place], mine[t, place]) for t in range(terms)],
            axis=0,
        )
        total = dot(halves[r], stacked).astype(jnp.bfloat16)
        for a in range(lefts):
            out_ref[a * rights + r] = total[a * width : (a + 1) * width]


def call(kernel, shape, operands, space, scratch=(), name=None, flops=0, limit=VMEM_LIMIT):
    spec = pl.BlockSpec(memory_space=space)
    return pl.pallas_call(
        kernel,
        out_shape=jax.ShapeDtypeStruct(shape, jnp.bfloat16),
        in_specs=[spec] * len(operands),
        out_specs=spec,
        scratch_shapes=list(scratch),
        compiler_params=pltpu.CompilerParams(vmem_limit_bytes=limit),
        cost_estimate=pl.CostEstimate(
            flops=flops, bytes_accessed=4 * 1024 * 1024, transcendentals=0
        ),
        name=name,
    )(*operands)


def shards(psi_first, psi_second, left_env, right_env, links):
    tiles, width, _ = psi_first.shape
    terms, lefts, _, _ = left_env.shape
    rights = right_env.shape[1]
    peers = lax.axis_size(SEC)
    every = peers * tiles
    swap = [(0, 1), (1, 0)]

    slabs = width // 2 // SLAB
    upper = (rights + 1) // 2
    core = lax.axis_index("core")

    other_links = lax.ppermute(links, "v", swap)
    pieces = call(
        cut_kernel,
        (peers * 2 * tiles, width),
        (psi_first, psi_second),
        pl.ANY,
        scratch=[
            pltpu.VMEM(psi_first.shape, jnp.bfloat16),
            pltpu.VMEM((slabs, 2 * tiles * SLAB, width), jnp.bfloat16),
            pltpu.SemaphoreType.DMA((CHUNKS,)),
            pltpu.SemaphoreType.DMA((slabs,)),
        ],
        name="cut",
        flops=400_000_000,
        limit=VMEM_WHOLE,
    )
    pieces = lax.all_to_all(pieces, SEC, split_axis=0, concat_axis=0, tiled=True)
    other_left = lax.ppermute(left_env, "v", swap)
    wanted = jnp.stack([links.reshape(peers, tiles), other_links.reshape(peers, tiles)], axis=1)
    hot = (wanted.reshape(2 * every, 1) == jnp.arange(every)[None, :]).astype(jnp.bfloat16)
    chosen = call(
        choose_kernel,
        (2 * every, 2 * width),
        (pieces, hot),
        pltpu.VMEM,
        scratch=[pltpu.VMEM((every, 2 * width), jnp.bfloat16)],
        name="choose",
        flops=700_000_000,
    )
    chosen, other_left = lax.optimization_barrier((chosen, other_left))
    arrived = lax.all_to_all(chosen, SEC, split_axis=0, concat_axis=0, tiled=True)
    near = lax.dynamic_slice_in_dim(right_env, core * (rights - upper), upper, 1)
    near = lax.ppermute(near, "v", swap)
    far = lax.ppermute(near, "core", swap)
    partial = call(
        apply_kernel,
        (tiles, width, width),
        (arrived, left_env, other_left, right_env, near, far),
        pltpu.VMEM,
        scratch=[
            pltpu.VMEM((2, lefts, width, rights * width), jnp.bfloat16),
            pltpu.VMEM((rights, lefts * width, 2 * terms * width), jnp.bfloat16),
        ],
        name="apply",
        flops=2_000_000_000,
    )
    quarters = lax.axis_size("q")
    parts = lax.all_to_all(partial, "q", split_axis=0, concat_axis=0, tiled=True)
    parts = parts.reshape(quarters, tiles // quarters, width, width)
    mine = jnp.sum(parts.astype(jnp.float32), axis=0).astype(jnp.bfloat16)
    own = lax.all_gather(mine, "q", axis=0, tiled=True)
    other = lax.ppermute(own, "v", swap)
    first = lax.axis_index("v") == 0
    return jnp.where(first, own, other), jnp.where(first, other, own)


def solution(mesh):
    ops, secs = mesh.devices.shape
    grid = Mesh(mesh.devices.reshape(ops // 2, 2, secs // 2, 2), ("q", "v", "chip", "core"))
    op, sec = ("q", "v"), SEC
    in_specs = (
        P(sec, None, None),
        P(sec, None, None),
        P(op, sec, None, None),
        P(op, None, None, None),
        P(op, None),
    )
    out_specs = (P(sec, None, None), P(sec, None, None))
    return jax.shard_map(shards, mesh=grid, in_specs=in_specs, out_specs=out_specs, check_vma=False)
```

time: 117 us -> 114 us (0.974)
  blocking collectives: 49.8 us -> 38.7 us
  waiting for transfers between devices: 23 us -> 30.8 us
  starting transfers between devices: 31.3 us -> 33.3 us
  local copies, waits for them, and re-layouts: 3.37 us -> 1.45 us
    all_gather x1, blocking collectives: 26.2 us -> 15.1 us  [shards(): own = lax.all_gather(mine, 'q', axis=0, tiled=True)]
    ppermute x0 -> x1, waiting for transfers between devices: none -> 7.74 us  [shards(): other = lax.ppermute(own, 'v', swap)]
    ppermute x0 -> x1, starting transfers between devices: none -> 2.01 us  [shards(): other = lax.ppermute(own, 'v', swap)]
  transfers between devices with their start and end apart: 6 -> 7, of which waited for: 4 -> 5; matrix products, arithmetic and copies ran while one was open for 2% -> 2% of each run, Pallas kernels for 2% -> 2%
where the time goes in v3:
time: 114 us
  blocking collectives  38.7 us (34%)
  starting transfers between devices  33.3 us (29%)
  waiting for transfers between devices  30.8 us (27%)
  Pallas kernels  6.67 us (6%)
  other arithmetic  2.17 us (2%)
  local copies, waits for them, and re-layouts  1.45 us (1%)
    all_to_all x1, blocking collectives, shards(): lax.all_to_all(partial, 'q', split_axis=0, concat_axis=0, tiled=True)  23.6 us
    all_gather x1, blocking collectives, shards(): own = lax.all_gather(mine, 'q', axis=0, tiled=True)  15.1 us
    ppermute x1, waiting for transfers between devices, shards(): near = lax.ppermute(near, 'v', swap)  13 us
    all_to_all x1, starting transfers between devices, shards(): lax.all_to_all(pieces, SEC, split_axis=0, concat_axis=0, tiled=True)  10.8 us
    all_to_all x1, starting transfers between devices, shards(): lax.all_to_all(chosen, SEC, split_axis=0, concat_axis=0, tiled=True)  10.1 us
    ppermute x1, waiting for transfers between devices, shards(): other = lax.ppermute(own, 'v', swap)  7.74 us
    pallas_call x3, Pallas kernels, call(): pl.pallas_call(kernel, out_shape=jax.ShapeDtypeStruct(shape, jnp.bfloat16...  6.67 us
    all_to_all x1, waiting for transfers between devices, shards(): lax.all_to_all(pieces, SEC, split_axis=0, concat_axis=0, tiled=True)  6.31 us
  transfers between devices with their start and end apart: 7, of which 5 were waited for; matrix products, arithmetic and copies ran while one was open for 2% of the time, Pallas kernels for 2%

profile of v3, /device:TPU:6, one launch (start us, length us, event | category | flops | bytes accessed | tf_op | source)
XLA Modules:
  0.0 113.8 jit_solution(11219313866109012525)
XLA Ops:
  0.6 2.2 %cut.1 = bf16[1536,128]{1,0:T(8,128)(2,1)} custom-call(bf16[12,128,128]{2,1,0:T(8,128)(2,1)} %first_ref.1, bf16[12,128,128]{2,1,0:T(8,128)(2,1)} %second_ref.1), custom_call_target="tpu_custom_call" | custom-call | flops 400000000 | bytes 4194304 | tf_op jit(solution)/shard_map/cut/pallas_call | solution.py:151
  2.9 10.8 %all-to-all-start = ((bf16[64,24,128]{2,1,0:T(8,128)(2,1)}), bf16[64,24,128]{2,1,0:T(8,128)(2,1)S(1)}, u32[]{:S(2)}, u32[]{:S(2)}) async-start(bf16[64,24,128]{2,1,0:T(8,128)(2,1)} %bitcast.8), calls=%async_computation | async-start | bytes 786432 | tf_op jit(solution)/shard_map/all_to_all | solution.py:193
  13.7 4.3 %collective-permute-start = (s32[1,768]{1,0:T(1,128)}, s32[1,768]{1,0:T(1,128)S(1)}, u32[]{:S(2)}, u32[]{:S(2)}) collective-permute-start(s32[1,768]{1,0:T(1,128)} %param.9), channel_id=1, source_target_pairs={{0,64},{64,0},{1,65},{65,1},{2,66},{66,2},{3,67},{67,3},{4,68},{68... | collective-permute-start | bytes 9224 | tf_op jit(solution)/shard_map/ppermute | solution.py:177
  18.0 1.9 %collective-permute-start.1 = (bf16[5,2,128,128]{3,2,1,0:T(8,128)(2,1)}, bf16[5,2,128,128]{3,2,1,0:T(8,128)(2,1)S(1)}, u32[]{:S(2)}, u32[]{:S(2)}) collective-permute-start(bf16[5,2,128,128]{3,2,1,0:T(8,128)(2,1)} %left_a.1), channel_id=1, source_target_pairs={{0,64},{64,0},{1,65},{65,1},{2,66},{66,2},{3,67},{67,3},{4,68},{68... | collective-permute-start | bytes 983048 | tf_op jit(solution)/shard_map/ppermute | solution.py:194
  19.9 0.7 reduce.1
  20.6 0.1 stack_reshape.6
  20.7 0.0 collective-permute-done
  20.7 0.1 stack_reshape.7
  20.9 0.1 copy.11
  20.9 0.1 eq.19
  21.0 0.5 fusion.hot_ref
  21.5 6.3 %all-to-all-done = bf16[64,24,128]{2,1,0:T(8,128)(2,1)S(1)} async-done(((bf16[64,24,128]{2,1,0:T(8,128)(2,1)}), bf16[64,24,128]{2,1,0:T(8,128)(2,1)S(1)}, u32[]{:S(2)}, u32[]{:S(2)}) %all-to-all-start) | async-done | bytes 393248 | tf_op jit(solution)/shard_map/all_to_all | solution.py:193
  27.8 0.0 copy-start.1
  27.8 1.9 %choose.1 = bf16[1536,256]{1,0:T(8,128)(2,1)} custom-call(bf16[1536,128]{1,0:T(8,128)(2,1)S(1)} %bitcast.5, bf16[1536,768]{1,0:T(8,128)(2,1)S(1)} %fusion.hot_ref), custom_call_target="tpu_custom_call" | custom-call | flops 700000000 | bytes 4194304 | tf_op jit(solution)/shard_map/choose/pallas_call | solution.py:151
  29.7 0.0 copy-start
  29.7 0.0 collective-permute-done.1.left_b
  29.7 10.1 %all-to-all-start.1 = ((bf16[64,24,256]{2,1,0:T(8,128)(2,1)}), bf16[64,24,256]{2,1,0:T(8,128)(2,1)S(1)}, u32[]{:S(2)}, u32[]{:S(2)}) async-start(bf16[64,24,256]{2,1,0:T(8,128)(2,1)} %bitcast.2), calls=%async_computation.1 | async-start | bytes 1572864 | tf_op jit(solution)/shard_map/all_to_all | solution.py:207
  39.9 1.1 constant_dynamic-slice_fusion
  41.0 2.2 %collective-permute-start.2 = (bf16[5,3,128,128]{3,2,1,0:T(8,128)(2,1)S(1)}, bf16[5,3,128,128]{3,2,1,0:T(8,128)(2,1)S(1)}, u32[]{:S(2)}, u32[]{:S(2)}) collective-permute-start(bf16[5,3,128,128]{3,2,1,0:T(8,128)(2,1)S(1)} %constant_dynamic-slice_fusion), channel_id=1, source_target_pairs={{0,64},{64,0},{1,65},{65,1},{2,66},{66,2},{3,67},{67,3},{4,68},{68... | collective-permute-start | bytes 1474568 | tf_op jit(solution)/shard_map/ppermute | solution.py:209
  43.2 13.0 %collective-permute-done.2.near_ref = bf16[5,3,128,128]{3,2,1,0:T(8,128)(2,1)S(1)} collective-permute-done((bf16[5,3,128,128]{3,2,1,0:T(8,128)(2,1)S(1)}, bf16[5,3,128,128]{3,2,1,0:T(8,128)(2,1)S(1)}, u32[]{:S(2)}, u32[]{:S(2)}) %collective-permute-start.2) | collective-permute-done | bytes 491552 | tf_op jit(solution)/shard_map/ppermute | solution.py:209
  56.1 1.9 %collective-permute-start.3 = (bf16[5,3,128,128]{3,2,1,0:T(8,128)(2,1)S(1)}, bf16[5,3,128,128]{3,2,1,0:T(8,128)(2,1)S(1)}, u32[]{:S(2)}, u32[]{:S(2)}) collective-permute-start(bf16[5,3,128,128]{3,2,1,0:T(8,128)(2,1)S(1)} %collective-permute-done.2.near_ref), channel_id=1, source_target_pairs={{0,1},{1,0},{2,3},{3,2},{4,5},{5,4},{6,7},{7,6},{8,9},{9,8},{10,11... | collective-permute-start | bytes 1474568 | tf_op jit(solution)/shard_map/ppermute | solution.py:210
  58.1 1.8 %collective-permute-done.3.far_ref = bf16[5,3,128,128]{3,2,1,0:T(8,128)(2,1)S(1)} collective-permute-done((bf16[5,3,128,128]{3,2,1,0:T(8,128)(2,1)S(1)}, bf16[5,3,128,128]{3,2,1,0:T(8,128)(2,1)S(1)}, u32[]{:S(2)}, u32[]{:S(2)}) %collective-permute-start.3) | collective-permute-done | bytes 491552 | tf_op jit(solution)/shard_map/ppermute | solution.py:210
  59.9 1.9 %all-to-all-done.1 = bf16[64,24,256]{2,1,0:T(8,128)(2,1)S(1)} async-done(((bf16[64,24,256]{2,1,0:T(8,128)(2,1)}), bf16[64,24,256]{2,1,0:T(8,128)(2,1)S(1)}, u32[]{:S(2)}, u32[]{:S(2)}) %all-to-all-start.1) | async-done | bytes 786464 | tf_op jit(solution)/shard_map/all_to_all | solution.py:207
  61.8 0.0 copy-done.1
  61.8 0.0 copy-done
  61.8 2.5 %apply.1 = bf16[12,128,128]{2,1,0:T(8,128)(2,1)S(1)} custom-call(bf16[1536,256]{1,0:T(8,128)(2,1)S(1)} %bitcast.6, bf16[5,2,128,128]{3,2,1,0:T(8,128)(2,1)S(1)} %copy-done.1, bf16[5,2,128,128]{3,2,1,0:T(8,128)(2,1)S(1)} %collective-permute-done.1.left_b, bf16[5,6,128,128]{3,2,1,0:T(8,128)(2,1)S(1)} %copy-done, ...), custom_call_target="tpu_custom_call" | custom-call | flops 2000000000 | bytes 4194304 | tf_op jit(solution)/shard_map/apply/pallas_call | solution.py:151
  64.4 23.6 %all_to_all.27 = bf16[12,128,128]{2,1,0:T(8,128)(2,1)S(1)} all-to-all(bf16[12,128,128]{2,1,0:T(8,128)(2,1)S(1)} %apply.1), channel_id=1, replica_groups=mesh['q'=4,'v'=2,'chip'=32,'core'=2] {'q'}, dimensions={0} | all-to-all | bytes 786432 | tf_op jit(solution)/shard_map/all_to_all | solution.py:224
  88.0 0.1 reduce_sum.12
  88.0 15.1 %all_gather.3 = bf16[12,128,128]{2,1,0:T(8,128)(2,1)S(1)} all-gather(bf16[3,128,128]{2,1,0:T(8,128)(2,1)S(1)} %reduce_sum.12), channel_id=1, replica_groups=mesh['q'=4,'v'=2,'chip'=32,'core'=2] {'q'}, dimensions={0}, use_global_device_ids=true | all-gather | bytes 491520 | tf_op jit(solution)/shard_map/all_gather | solution.py:227
  103.2 2.0 %collective-permute-start.4 = (bf16[12,128,128]{2,1,0:T(8,128)(2,1)S(1)}, bf16[12,128,128]{2,1,0:T(8,128)(2,1)S(1)}, u32[]{:S(2)}, u32[]{:S(2)}) collective-permute-start(bf16[12,128,128]{2,1,0:T(8,128)(2,1)S(1)} %all_gather.3), channel_id=1, source_target_pairs={{0,64},{64,0},{1,65},{65,1},{2,66},{66,2},{3,67},{67,3},{4,68},{68... | collective-permute-start | bytes 1179656 | tf_op jit(solution)/shard_map/ppermute | solution.py:228
  105.2 7.7 %collective-permute-done.4 = bf16[12,128,128]{2,1,0:T(8,128)(2,1)S(1)} collective-permute-done((bf16[12,128,128]{2,1,0:T(8,128)(2,1)S(1)}, bf16[12,128,128]{2,1,0:T(8,128)(2,1)S(1)}, u32[]{:S(2)}, u32[]{:S(2)}) %collective-permute-start.4) | collective-permute-done | bytes 393248 | tf_op jit(solution)/shard_map/ppermute | solution.py:228
  112.9 0.9 broadcast_select_fusion
  (2 shorter events, 0.0 us)
Async XLA Ops:
  2.9 25.0 %all-to-all-start = ((bf16[64,24,128]{2,1,0:T(8,128)(2,1)}), bf16[64,24,128]{2,1,0:T(8,128)(2,1)S(1)}, u32[]{:S(2)}, u32[]{:S(2)}) async-start(bf16[64,24,128]{2,1,0:T(8,128)(2,1)} %bitcast.8), calls=%async_computation | async-start | bytes 786432 | tf_op jit(solution)/shard_map/all_to_all | solution.py:193
  13.7 7.0 %collective-permute-start = (s32[1,768]{1,0:T(1,128)}, s32[1,768]{1,0:T(1,128)S(1)}, u32[]{:S(2)}, u32[]{:S(2)}) collective-permute-start(s32[1,768]{1,0:T(1,128)} %param.9), channel_id=1, source_target_pairs={{0,64},{64,0},{1,65},{65,1},{2,66},{66,2},{3,67},{67,3},{4,68},{68... | collective-permute-start | bytes 9224 | tf_op jit(solution)/shard_map/ppermute | solution.py:177
  18.0 11.8 %collective-permute-start.1 = (bf16[5,2,128,128]{3,2,1,0:T(8,128)(2,1)}, bf16[5,2,128,128]{3,2,1,0:T(8,128)(2,1)S(1)}, u32[]{:S(2)}, u32[]{:S(2)}) collective-permute-start(bf16[5,2,128,128]{3,2,1,0:T(8,128)(2,1)} %left_a.1), channel_id=1, source_target_pairs={{0,64},{64,0},{1,65},{65,1},{2,66},{66,2},{3,67},{67,3},{4,68},{68... | collective-permute-start | bytes 983048 | tf_op jit(solution)/shard_map/ppermute | solution.py:194
  27.8 34.0 %copy-start.1 = (bf16[5,2,128,128]{3,2,1,0:T(8,128)(2,1)S(1)}, bf16[5,2,128,128]{3,2,1,0:T(8,128)(2,1)}, u32[]{:S(2)}) copy-start(bf16[5,2,128,128]{3,2,1,0:T(8,128)(2,1)} %left_a.1) | copy-start | bytes 983044
  29.7 32.1 %copy-start = (bf16[5,6,128,128]{3,2,1,0:T(8,128)(2,1)S(1)}, bf16[5,6,128,128]{3,2,1,0:T(8,128)(2,1)}, u32[]{:S(2)}) copy-start(bf16[5,6,128,128]{3,2,1,0:T(8,128)(2,1)} %right_a.1) | copy-start | bytes 2949124
  29.7 32.1 %all-to-all-start.1 = ((bf16[64,24,256]{2,1,0:T(8,128)(2,1)}), bf16[64,24,256]{2,1,0:T(8,128)(2,1)S(1)}, u32[]{:S(2)}, u32[]{:S(2)}) async-start(bf16[64,24,256]{2,1,0:T(8,128)(2,1)} %bitcast.2), calls=%async_computation.1 | async-start | bytes 1572864 | tf_op jit(solution)/shard_map/all_to_all | solution.py:207
  41.0 15.2 %collective-permute-start.2 = (bf16[5,3,128,128]{3,2,1,0:T(8,128)(2,1)S(1)}, bf16[5,3,128,128]{3,2,1,0:T(8,128)(2,1)S(1)}, u32[]{:S(2)}, u32[]{:S(2)}) collective-permute-start(bf16[5,3,128,128]{3,2,1,0:T(8,128)(2,1)S(1)} %constant_dynamic-slice_fusion), channel_id=1, source_target_pairs={{0,64},{64,0},{1,65},{65,1},{2,66},{66,2},{3,67},{67,3},{4,68},{68... | collective-permute-start | bytes 1474568 | tf_op jit(solution)/shard_map/ppermute | solution.py:209
  56.1 3.7 %collective-permute-start.3 = (bf16[5,3,128,128]{3,2,1,0:T(8,128)(2,1)S(1)}, bf16[5,3,128,128]{3,2,1,0:T(8,128)(2,1)S(1)}, u32[]{:S(2)}, u32[]{:S(2)}) collective-permute-start(bf16[5,3,128,128]{3,2,1,0:T(8,128)(2,1)S(1)} %collective-permute-done.2.near_ref), channel_id=1, source_target_pairs={{0,1},{1,0},{2,3},{3,2},{4,5},{5,4},{6,7},{7,6},{8,9},{9,8},{10,11... | collective-permute-start | bytes 1474568 | tf_op jit(solution)/shard_map/ppermute | solution.py:210
  103.2 9.8 %collective-permute-start.4 = (bf16[12,128,128]{2,1,0:T(8,128)(2,1)S(1)}, bf16[12,128,128]{2,1,0:T(8,128)(2,1)S(1)}, u32[]{:S(2)}, u32[]{:S(2)}) collective-permute-start(bf16[12,128,128]{2,1,0:T(8,128)(2,1)S(1)} %all_gather.3), channel_id=1, source_target_pairs={{0,64},{64,0},{1,65},{65,1},{2,66},{66,2},{3,67},{67,3},{4,68},{68... | collective-permute-start | bytes 1179656 | tf_op jit(solution)/shard_map/ppermute | solution.py:228

commit v4 on v3

--- a/solution.py
+++ b/solution.py
@@ -1,3 +1,5 @@
+import functools
+
 import jax
 import jax.numpy as jnp
 from jax import lax
@@ -6,9 +8,8 @@
 from jax.sharding import Mesh, PartitionSpec as P
 
 VMEM_LIMIT = 30 * 1024 * 1024
-VMEM_WHOLE = 60 * 1024 * 1024
 SLAB = 16
-CHUNKS = 4
+STEPS = 6
 SEC = ("chip", "core")
 
 
@@ -28,61 +29,27 @@
     )
 
 
-def cut_kernel(first_ref, second_ref, out_ref, held, cut, fetch_sems, send_sems):
-    tiles, width, _ = first_ref.shape
-    half = width // 2
-    slabs = half // SLAB
-    rows = 2 * tiles * SLAB
-    vector = lax.axis_index("v")
-
-    def fetch(source, chunk):
-        span = pl.ds(chunk * (tiles // CHUNKS), tiles // CHUNKS)
-        return pltpu.make_async_copy(source.at[span], held.at[span], fetch_sems.at[chunk])
-
-    def send(slab):
-        return pltpu.make_async_copy(
-            cut.at[slab], out_ref.at[pl.ds(slab * rows, rows)], send_sems.at[slab]
-        )
-
-    for number, source in enumerate((first_ref, second_ref)):
-
-        @pl.when(vector == number)
-        def _():
-            for chunk in range(CHUNKS):
-                fetch(source, chunk).start()
-
-    unit = lax.broadcasted_iota(jnp.int32, (1, rows), 1)
-    place, unit = unit % SLAB, unit // SLAB
-    target = place * 2 * tiles + unit % tiles * 2 + unit // tiles
-    order = ones_where(lax.broadcasted_iota(jnp.int32, (rows, rows), 0) == target)
-    for chunk in range(CHUNKS):
-        fetch(first_ref, chunk).wait()
-    for slab in range(slabs):
-        starts = [top * half + slab * SLAB for top in range(2)]
-        block = jnp.concatenate(
-            [held[k, start : start + SLAB, :] for start in starts for k in range(tiles)], axis=0
-        )
-        cut[slab] = dot(order, block).astype(jnp.bfloat16)
-        send(slab).start()
-    for slab in range(slabs):
-        send(slab).wait()
-
-
-def choose_kernel(pieces_ref, hot_ref, out_ref, wide):
+def choose_kernel(pieces_ref, hot_ref, out_ref, wide, block, sems):
     count = 96
     lanes = pieces_ref.shape[1]
     row, column = iotas(count, 2 * count)
     parity = [ones_where(column == 2 * row + top) for top in range(2)]
     for b in range(pieces_ref.shape[0] // (2 * count)):
-        block = pieces_ref[2 * count * b : 2 * count * (b + 1), :]
+        pair = pieces_ref[2 * count * b : 2 * count * (b + 1), :]
         for top in range(2):
-            picked = dot(parity[top], block).astype(jnp.bfloat16)
+            picked = dot(parity[top], pair).astype(jnp.bfloat16)
             wide[count * b : count * (b + 1), top * lanes : (top + 1) * lanes] = picked
-    step = 256
-    for m in range(hot_ref.shape[0] // step):
-        out_ref[m * step : (m + 1) * step, :] = dot(
-            hot_ref[m * step : (m + 1) * step, :], wide[...]
-        ).astype(jnp.bfloat16)
+    steps, step, _ = block.shape
+
+    def send(m):
+        return pltpu.make_async_copy(block.at[m], out_ref.at[pl.ds(m * step, step)], sems.at[m])
+
+    for m in range(steps):
+        hot = hot_ref[m * step : (m + 1) * step, :]
+        block[m] = dot(hot, wide[...]).astype(jnp.bfloat16)
+        send(m).start()
+    for m in range(steps):
+        send(m).wait()
 
 
 def apply_kernel(
@@ -125,13 +92,17 @@
     for g, left in enumerate((left_a, left_b)):
         for a in range(lefts):
             stacked = jnp.concatenate([left[t, a] for t in range(terms)], axis=0)
-            product = dot(stacked, tiles[g, a]).astype(jnp.bfloat16)
-            for t in range(terms):
-                for r in range(rights):
-                    column = (g * terms + t) * width
-                    halves[r, a * width : (a + 1) * width, column : column + width] = product[
-                        t * width : (t + 1) * width, r * width : (r + 1) * width
-                    ]
+            for pair in range(rights // 2):
+                span = slice(2 * pair * width, 2 * (pair + 1) * width)
+                product = dot(stacked, tiles[g, a, :, span]).astype(jnp.bfloat16)
+                for t in range(terms):
+                    for side in range(2):
+                        column = (g * terms + t) * width
+                        halves[
+                            2 * pair + side, a * width : (a + 1) * width, column : column + width
+                        ] = product[
+                            t * width : (t + 1) * width, side * width : (side + 1) * width
+                        ]
     for r in range(rights):
         side = 0 if r < upper else 1
         place = r - side * (rights - upper)
@@ -146,13 +117,50 @@
             out_ref[a * rights + r] = total[a * width : (a + 1) * width]
 
 
-def call(kernel, shape, operands, space, scratch=(), name=None, flops=0, limit=VMEM_LIMIT):
+def place_kernel(number, data_ref, *refs):
+    first_ref, second_ref, sems = refs[-3:]
+    turn = (lax.axis_index("v") + number) % 2
+    chunks = sems.shape[0]
+    count = data_ref.shape[0] // chunks
+
+    def move(target, chunk):
+        span = pl.ds(chunk * count, count)
+        return pltpu.make_async_copy(data_ref.at[span], target.at[span], sems.at[chunk])
+
+    for side, target in enumerate((first_ref, second_ref)):
+
+        @pl.when(turn == side)
+        def _():
+            for chunk in range(chunks):
+                move(target, chunk).start()
+
+    for chunk in range(chunks):
+        move(first_ref, chunk).wait()
+
+
+def place(number, data, *ends):
+    end = jax.ShapeDtypeStruct(data.shape, jnp.bfloat16)
+    return pl.pallas_call(
+        functools.partial(place_kernel, number),
+        out_shape=(end, end),
+        in_specs=[pl.BlockSpec(memory_space=pltpu.VMEM)]
+        + [pl.BlockSpec(memory_space=pl.ANY)] * len(ends),
+        out_specs=(pl.BlockSpec(memory_space=pl.ANY),) * 2,
+        scratch_shapes=[pltpu.SemaphoreType.DMA((4,))],
+        input_output_aliases={1: 0, 2: 1} if ends else {},
+        compiler_params=pltpu.CompilerParams(vmem_limit_bytes=VMEM_LIMIT),
+        name="place",
+    )(data, *ends)
+
+
+def call(kernel, shape, operands, space, scratch=(), name=None, flops=0, limit=VMEM_LIMIT, out_space=None):
     spec = pl.BlockSpec(memory_space=space)
+    out_spec = pl.BlockSpec(memory_space=out_space or space)
     return pl.pallas_call(
         kernel,
         out_shape=jax.ShapeDtypeStruct(shape, jnp.bfloat16),
         in_specs=[spec] * len(operands),
-        out_specs=spec,
+        out_specs=out_spec,
         scratch_shapes=list(scratch),
         compiler_params=pltpu.CompilerParams(vmem_limit_bytes=limit),
         cost_estimate=pl.CostEstimate(
@@ -170,26 +178,13 @@
     every = peers * tiles
     swap = [(0, 1), (1, 0)]
 
-    slabs = width // 2 // SLAB
     upper = (rights + 1) // 2
     core = lax.axis_index("core")
 
     other_links = lax.ppermute(links, "v", swap)
-    pieces = call(
-        cut_kernel,
-        (peers * 2 * tiles, width),
-        (psi_first, psi_second),
-        pl.ANY,
-        scratch=[
-            pltpu.VMEM(psi_first.shape, jnp.bfloat16),
-            pltpu.VMEM((slabs, 2 * tiles * SLAB, width), jnp.bfloat16),
-            pltpu.SemaphoreType.DMA((CHUNKS,)),
-            pltpu.SemaphoreType.DMA((slabs,)),
-        ],
-        name="cut",
-        flops=400_000_000,
-        limit=VMEM_WHOLE,
-    )
+    chosen_psi = jnp.where(lax.axis_index("v") == 0, psi_first, psi_second)
+    pieces = chosen_psi.reshape(tiles, 2, width // 2, width).transpose(2, 0, 1, 3)
+    pieces = pieces.reshape(peers * 2 * tiles, width)
     pieces = lax.all_to_all(pieces, SEC, split_axis=0, concat_axis=0, tiled=True)
     other_left = lax.ppermute(left_env, "v", swap)
     wanted = jnp.stack([links.reshape(peers, tiles), other_links.reshape(peers, tiles)], axis=1)
@@ -199,8 +194,13 @@
         (2 * every, 2 * width),
         (pieces, hot),
         pltpu.VMEM,
-        scratch=[pltpu.VMEM((every, 2 * width), jnp.bfloat16)],
+        scratch=[
+            pltpu.VMEM((every, 2 * width), jnp.bfloat16),
+            pltpu.VMEM((STEPS, 2 * every // STEPS, 2 * width), jnp.bfloat16),
+            pltpu.SemaphoreType.DMA((STEPS,)),
+        ],
         name="choose",
+        out_space=pl.ANY,
         flops=700_000_000,
     )
     chosen, other_left = lax.optimization_barrier((chosen, other_left))
@@ -226,8 +226,7 @@
     mine = jnp.sum(parts.astype(jnp.float32), axis=0).astype(jnp.bfloat16)
     own = lax.all_gather(mine, "q", axis=0, tiled=True)
     other = lax.ppermute(own, "v", swap)
-    first = lax.axis_index("v") == 0
-    return jnp.where(first, own, other), jnp.where(first, other, own)
+    return place(1, other, *place(0, own))
 
 
 def solution(mesh):

time: 114 us -> 114 us (level)
  local copies, waits for them, and re-layouts: 1.45 us -> 2.61 us
    pallas_call x3 -> x2, Pallas kernels: 6.67 us -> 4.31 us  [call(): pl.pallas_call(kernel, out_shape=jax.ShapeDtypeStruct(shape, jnp.bfloat16...]
    pallas_call x0 -> x2, Pallas kernels: none -> 1.56 us  [place(): pl.pallas_call(functools.partial(place_kernel, number), out_shape=(end, e...]
    transpose x0 -> x1, local copies, waits for them, and re-layouts: none -> 1.15 us  [shards(): chosen_psi.reshape(tiles, 2, width // 2, width).transpose(2, 0, 1, 3)]
where the time goes in v4:
time: 114 us
  blocking collectives  38.8 us (34%)
  starting transfers between devices  33.2 us (29%)
  waiting for transfers between devices  30.6 us (27%)
  Pallas kernels  5.87 us (5%)
  local copies, waits for them, and re-layouts  2.61 us (2%)
  other arithmetic  1.64 us (1%)
    all_to_all x1, blocking collectives, shards(): lax.all_to_all(partial, 'q', split_axis=0, concat_axis=0, tiled=True)  23.6 us
    all_gather x1, blocking collectives, shards(): own = lax.all_gather(mine, 'q', axis=0, tiled=True)  15.1 us
    ppermute x1, waiting for transfers between devices, shards(): near = lax.ppermute(near, 'v', swap)  13 us
    all_to_all x1, starting transfers between devices, shards(): lax.all_to_all(pieces, SEC, split_axis=0, concat_axis=0, tiled=True)  10.8 us
    all_to_all x1, starting transfers between devices, shards(): lax.all_to_all(chosen, SEC, split_axis=0, concat_axis=0, tiled=True)  10.1 us
    all_to_all x1, waiting for transfers between devices, shards(): lax.all_to_all(pieces, SEC, split_axis=0, concat_axis=0, tiled=True)  6.98 us
    ppermute x1, waiting for transfers between devices, shards(): other = lax.ppermute(own, 'v', swap)  6.9 us
    pallas_call x2, Pallas kernels, call(): pl.pallas_call(kernel, out_shape=jax.ShapeDtypeStruct(shape, jnp.bfloat16...  4.31 us
  transfers between devices with their start and end apart: 7, of which 5 were waited for; matrix products, arithmetic and copies ran while one was open for 2% of the time, Pallas kernels for 2%

profile of v4, /device:TPU:6, one launch (start us, length us, event | category | flops | bytes accessed | tf_op | source)
XLA Modules:
  0.0 113.5 jit_solution(4227645905132460477)
XLA Ops:
  0.6 0.0 copy-start.2
  0.6 0.0 copy-start.1
  0.7 1.1 broadcast_select_fusion
  1.8 1.2 %copy.16 = bf16[64,12,2,128]{3,2,1,0:T(2,128)(2,1)} copy(bf16[64,12,2,128]{3,0,2,1:T(8,128)(2,1)S(1)} %bitcast.11) | data formatting | bytes 786432 | tf_op jit(solution)/shard_map/transpose | solution.py:186
  2.9 10.8 %all-to-all-start = ((bf16[64,24,128]{2,1,0:T(8,128)(2,1)}), bf16[64,24,128]{2,1,0:T(8,128)(2,1)S(1)}, u32[]{:S(2)}, u32[]{:S(2)}) async-start(bf16[64,24,128]{2,1,0:T(8,128)(2,1)} %bitcast.2), calls=%async_computation | async-start | bytes 786432 | tf_op jit(solution)/shard_map/all_to_all | solution.py:188
  13.7 0.0 copy-done.2
  13.7 4.3 %collective-permute-start = (s32[1,768]{1,0:T(1,128)S(1)}, s32[1,768]{1,0:T(1,128)S(1)}, u32[]{:S(2)}, u32[]{:S(2)}) collective-permute-start(s32[1,768]{1,0:T(1,128)S(1)} %copy-done.2), channel_id=1, source_target_pairs={{0,64},{64,0},{1,65},{65,1},{2,66},{66,2},{3,67},{67,3},{4,68},{68... | collective-permute-start | bytes 9224 | tf_op jit(solution)/shard_map/ppermute | solution.py:184
  18.0 0.0 copy-done.1
  18.0 1.9 %collective-permute-start.1 = (bf16[5,2,128,128]{3,2,1,0:T(8,128)(2,1)S(1)}, bf16[5,2,128,128]{3,2,1,0:T(8,128)(2,1)S(1)}, u32[]{:S(2)}, u32[]{:S(2)}) collective-permute-start(bf16[5,2,128,128]{3,2,1,0:T(8,128)(2,1)S(1)} %copy-done.1), channel_id=1, source_target_pairs={{0,64},{64,0},{1,65},{65,1},{2,66},{66,2},{3,67},{67,3},{4,68},{68... | collective-permute-start | bytes 983048 | tf_op jit(solution)/shard_map/ppermute | solution.py:189
  20.0 0.1 stack_reshape.6
  20.1 0.0 collective-permute-done
  20.1 0.1 stack_reshape.7
  20.2 0.1 copy.17
  20.3 0.1 eq.19
  20.4 0.5 fusion.hot_ref
  20.9 7.0 %all-to-all-done = bf16[64,24,128]{2,1,0:T(8,128)(2,1)S(1)} async-done(((bf16[64,24,128]{2,1,0:T(8,128)(2,1)}), bf16[64,24,128]{2,1,0:T(8,128)(2,1)S(1)}, u32[]{:S(2)}, u32[]{:S(2)}) %all-to-all-start) | async-done | bytes 393248 | tf_op jit(solution)/shard_map/all_to_all | solution.py:188
  27.9 1.8 %choose.1 = bf16[1536,256]{1,0:T(8,128)(2,1)} custom-call(bf16[1536,128]{1,0:T(8,128)(2,1)S(1)} %bitcast.8, bf16[1536,768]{1,0:T(8,128)(2,1)S(1)} %fusion.hot_ref), custom_call_target="tpu_custom_call" | custom-call | flops 700000000 | bytes 4194304 | tf_op jit(solution)/shard_map/choose/pallas_call | solution.py:159
  29.6 0.0 copy-start
  29.7 0.0 collective-permute-done.1.left_b
  29.7 10.1 %all-to-all-start.1 = ((bf16[64,24,256]{2,1,0:T(8,128)(2,1)}), bf16[64,24,256]{2,1,0:T(8,128)(2,1)S(1)}, u32[]{:S(2)}, u32[]{:S(2)}) async-start(bf16[64,24,256]{2,1,0:T(8,128)(2,1)} %bitcast.4), calls=%async_computation.1 | async-start | bytes 1572864 | tf_op jit(solution)/shard_map/all_to_all | solution.py:207
  39.7 1.1 constant_dynamic-slice_fusion
  40.8 2.2 %collective-permute-start.2 = (bf16[5,3,128,128]{3,2,1,0:T(8,128)(2,1)S(1)}, bf16[5,3,128,128]{3,2,1,0:T(8,128)(2,1)S(1)}, u32[]{:S(2)}, u32[]{:S(2)}) collective-permute-start(bf16[5,3,128,128]{3,2,1,0:T(8,128)(2,1)S(1)} %constant_dynamic-slice_fusion), channel_id=1, source_target_pairs={{0,64},{64,0},{1,65},{65,1},{2,66},{66,2},{3,67},{67,3},{4,68},{68... | collective-permute-start | bytes 1474568 | tf_op jit(solution)/shard_map/ppermute | solution.py:209
  43.0 13.0 %collective-permute-done.2.near_ref = bf16[5,3,128,128]{3,2,1,0:T(8,128)(2,1)S(1)} collective-permute-done((bf16[5,3,128,128]{3,2,1,0:T(8,128)(2,1)S(1)}, bf16[5,3,128,128]{3,2,1,0:T(8,128)(2,1)S(1)}, u32[]{:S(2)}, u32[]{:S(2)}) %collective-permute-start.2) | collective-permute-done | bytes 491552 | tf_op jit(solution)/shard_map/ppermute | solution.py:209
  56.0 1.9 %collective-permute-start.3 = (bf16[5,3,128,128]{3,2,1,0:T(8,128)(2,1)S(1)}, bf16[5,3,128,128]{3,2,1,0:T(8,128)(2,1)S(1)}, u32[]{:S(2)}, u32[]{:S(2)}) collective-permute-start(bf16[5,3,128,128]{3,2,1,0:T(8,128)(2,1)S(1)} %collective-permute-done.2.near_ref), channel_id=1, source_target_pairs={{0,1},{1,0},{2,3},{3,2},{4,5},{5,4},{6,7},{7,6},{8,9},{9,8},{10,11... | collective-permute-start | bytes 1474568 | tf_op jit(solution)/shard_map/ppermute | solution.py:210
  57.9 1.8 %collective-permute-done.3.far_ref = bf16[5,3,128,128]{3,2,1,0:T(8,128)(2,1)S(1)} collective-permute-done((bf16[5,3,128,128]{3,2,1,0:T(8,128)(2,1)S(1)}, bf16[5,3,128,128]{3,2,1,0:T(8,128)(2,1)S(1)}, u32[]{:S(2)}, u32[]{:S(2)}) %collective-permute-start.3) | collective-permute-done | bytes 491552 | tf_op jit(solution)/shard_map/ppermute | solution.py:210
  59.7 1.9 %all-to-all-done.1 = bf16[64,24,256]{2,1,0:T(8,128)(2,1)S(1)} async-done(((bf16[64,24,256]{2,1,0:T(8,128)(2,1)}), bf16[64,24,256]{2,1,0:T(8,128)(2,1)S(1)}, u32[]{:S(2)}, u32[]{:S(2)}) %all-to-all-start.1) | async-done | bytes 786464 | tf_op jit(solution)/shard_map/all_to_all | solution.py:207
  61.6 0.0 copy-done
  61.6 2.5 %apply.1 = bf16[12,128,128]{2,1,0:T(8,128)(2,1)S(1)} custom-call(bf16[1536,256]{1,0:T(8,128)(2,1)S(1)} %bitcast.9, bf16[5,2,128,128]{3,2,1,0:T(8,128)(2,1)S(1)} %copy-done.1, bf16[5,2,128,128]{3,2,1,0:T(8,128)(2,1)S(1)} %collective-permute-done.1.left_b, bf16[5,6,128,128]{3,2,1,0:T(8,128)(2,1)S(1)} %copy-done, ...), custom_call_target="tpu_custom_call" | custom-call | flops 2000000000 | bytes 4194304 | tf_op jit(solution)/shard_map/apply/pallas_call | solution.py:159
  64.2 23.6 %all_to_all.27 = bf16[12,128,128]{2,1,0:T(8,128)(2,1)S(1)} all-to-all(bf16[12,128,128]{2,1,0:T(8,128)(2,1)S(1)} %apply.1), channel_id=1, replica_groups=mesh['q'=4,'v'=2,'chip'=32,'core'=2] {'q'}, dimensions={0} | all-to-all | bytes 786432 | tf_op jit(solution)/shard_map/all_to_all | solution.py:224
  87.8 0.1 reduce_sum.12
  87.9 15.1 %all_gather.3.data_ref = bf16[12,128,128]{2,1,0:T(8,128)(2,1)S(1)} all-gather(bf16[3,128,128]{2,1,0:T(8,128)(2,1)S(1)} %reduce_sum.12), channel_id=1, replica_groups=mesh['q'=4,'v'=2,'chip'=32,'core'=2] {'q'}, dimensions={0}, use_global_device_ids=true | all-gather | bytes 491520 | tf_op jit(solution)/shard_map/all_gather | solution.py:227
  103.0 2.0 %collective-permute-start.4 = (bf16[12,128,128]{2,1,0:T(8,128)(2,1)S(1)}, bf16[12,128,128]{2,1,0:T(8,128)(2,1)S(1)}, u32[]{:S(2)}, u32[]{:S(2)}) collective-permute-start(bf16[12,128,128]{2,1,0:T(8,128)(2,1)S(1)} %all_gather.3.data_ref), channel_id=1, source_target_pairs={{0,64},{64,0},{1,65},{65,1},{2,66},{66,2},{3,67},{67,3},{4,68},{68... | collective-permute-start | bytes 1179656 | tf_op jit(solution)/shard_map/ppermute | solution.py:228
  105.1 0.8 place.2
  105.9 6.9 %collective-permute-done.4.data_ref = bf16[12,128,128]{2,1,0:T(8,128)(2,1)S(1)} collective-permute-done((bf16[12,128,128]{2,1,0:T(8,128)(2,1)S(1)}, bf16[12,128,128]{2,1,0:T(8,128)(2,1)S(1)}, u32[]{:S(2)}, u32[]{:S(2)}) %collective-permute-start.4) | collective-permute-done | bytes 393248 | tf_op jit(solution)/shard_map/ppermute | solution.py:228
  112.8 0.8 place.3
  (3 shorter events, 0.0 us)
Async XLA Ops:
  0.6 13.1 %copy-start.2 = (s32[1,768]{1,0:T(1,128)S(1)}, s32[1,768]{1,0:T(1,128)}, u32[]{:S(2)}) copy-start(s32[1,768]{1,0:T(1,128)} %param.9) | copy-start | bytes 9220
  0.6 17.4 %copy-start.1 = (bf16[5,2,128,128]{3,2,1,0:T(8,128)(2,1)S(1)}, bf16[5,2,128,128]{3,2,1,0:T(8,128)(2,1)}, u32[]{:S(2)}) copy-start(bf16[5,2,128,128]{3,2,1,0:T(8,128)(2,1)} %left_a.1) | copy-start | bytes 983044
  2.9 25.0 %all-to-all-start = ((bf16[64,24,128]{2,1,0:T(8,128)(2,1)}), bf16[64,24,128]{2,1,0:T(8,128)(2,1)S(1)}, u32[]{:S(2)}, u32[]{:S(2)}) async-start(bf16[64,24,128]{2,1,0:T(8,128)(2,1)} %bitcast.2), calls=%async_computation | async-start | bytes 786432 | tf_op jit(solution)/shard_map/all_to_all | solution.py:188
  13.7 6.4 %collective-permute-start = (s32[1,768]{1,0:T(1,128)S(1)}, s32[1,768]{1,0:T(1,128)S(1)}, u32[]{:S(2)}, u32[]{:S(2)}) collective-permute-start(s32[1,768]{1,0:T(1,128)S(1)} %copy-done.2), channel_id=1, source_target_pairs={{0,64},{64,0},{1,65},{65,1},{2,66},{66,2},{3,67},{67,3},{4,68},{68... | collective-permute-start | bytes 9224 | tf_op jit(solution)/shard_map/ppermute | solution.py:184
  18.0 11.6 %collective-permute-start.1 = (bf16[5,2,128,128]{3,2,1,0:T(8,128)(2,1)S(1)}, bf16[5,2,128,128]{3,2,1,0:T(8,128)(2,1)S(1)}, u32[]{:S(2)}, u32[]{:S(2)}) collective-permute-start(bf16[5,2,128,128]{3,2,1,0:T(8,128)(2,1)S(1)} %copy-done.1), channel_id=1, source_target_pairs={{0,64},{64,0},{1,65},{65,1},{2,66},{66,2},{3,67},{67,3},{4,68},{68... | collective-permute-start | bytes 983048 | tf_op jit(solution)/shard_map/ppermute | solution.py:189
  29.6 32.0 %copy-start = (bf16[5,6,128,128]{3,2,1,0:T(8,128)(2,1)S(1)}, bf16[5,6,128,128]{3,2,1,0:T(8,128)(2,1)}, u32[]{:S(2)}) copy-start(bf16[5,6,128,128]{3,2,1,0:T(8,128)(2,1)} %right_a.1) | copy-start | bytes 2949124
  29.7 32.0 %all-to-all-start.1 = ((bf16[64,24,256]{2,1,0:T(8,128)(2,1)}), bf16[64,24,256]{2,1,0:T(8,128)(2,1)S(1)}, u32[]{:S(2)}, u32[]{:S(2)}) async-start(bf16[64,24,256]{2,1,0:T(8,128)(2,1)} %bitcast.4), calls=%async_computation.1 | async-start | bytes 1572864 | tf_op jit(solution)/shard_map/all_to_all | solution.py:207
  40.8 15.2 %collective-permute-start.2 = (bf16[5,3,128,128]{3,2,1,0:T(8,128)(2,1)S(1)}, bf16[5,3,128,128]{3,2,1,0:T(8,128)(2,1)S(1)}, u32[]{:S(2)}, u32[]{:S(2)}) collective-permute-start(bf16[5,3,128,128]{3,2,1,0:T(8,128)(2,1)S(1)} %constant_dynamic-slice_fusion), channel_id=1, source_target_pairs={{0,64},{64,0},{1,65},{65,1},{2,66},{66,2},{3,67},{67,3},{4,68},{68... | collective-permute-start | bytes 1474568 | tf_op jit(solution)/shard_map/ppermute | solution.py:209
  56.0 3.7 %collective-permute-start.3 = (bf16[5,3,128,128]{3,2,1,0:T(8,128)(2,1)S(1)}, bf16[5,3,128,128]{3,2,1,0:T(8,128)(2,1)S(1)}, u32[]{:S(2)}, u32[]{:S(2)}) collective-permute-start(bf16[5,3,128,128]{3,2,1,0:T(8,128)(2,1)S(1)} %collective-permute-done.2.near_ref), channel_id=1, source_target_pairs={{0,1},{1,0},{2,3},{3,2},{4,5},{5,4},{6,7},{7,6},{8,9},{9,8},{10,11... | collective-permute-start | bytes 1474568 | tf_op jit(solution)/shard_map/ppermute | solution.py:210
  103.0 9.7 %collective-permute-start.4 = (bf16[12,128,128]{2,1,0:T(8,128)(2,1)S(1)}, bf16[12,128,128]{2,1,0:T(8,128)(2,1)S(1)}, u32[]{:S(2)}, u32[]{:S(2)}) collective-permute-start(bf16[12,128,128]{2,1,0:T(8,128)(2,1)S(1)} %all_gather.3.data_ref), channel_id=1, source_target_pairs={{0,64},{64,0},{1,65},{65,1},{2,66},{66,2},{3,67},{67,3},{4,68},{68... | collective-permute-start | bytes 1179656 | tf_op jit(solution)/shard_map/ppermute | solution.py:228

commit v5 on v4

--- a/solution.py
+++ b/solution.py
@@ -221,10 +221,18 @@
         flops=2_000_000_000,
     )
     quarters = lax.axis_size("q")
-    parts = lax.all_to_all(partial, "q", split_axis=0, concat_axis=0, tiled=True)
+    axes = ("q", "v", "core")
+    sets = [
+        [(q * 2 + v) * 2 + c for q in (range(quarters) if c == 0 else reversed(range(quarters)))]
+        for v in range(2)
+        for c in range(2)
+    ]
+    parts = lax.all_to_all(
+        partial, axes, split_axis=0, concat_axis=0, tiled=True, axis_index_groups=sets
+    )
     parts = parts.reshape(quarters, tiles // quarters, width, width)
     mine = jnp.sum(parts.astype(jnp.float32), axis=0).astype(jnp.bfloat16)
-    own = lax.all_gather(mine, "q", axis=0, tiled=True)
+    own = lax.all_gather(mine, axes, axis=0, tiled=True, axis_index_groups=sets)
     other = lax.ppermute(own, "v", swap)
     return place(1, other, *place(0, own))
 

time: 114 us -> 114 us (level)
  blocking collectives: 38.8 us -> 36.8 us
  starting transfers between devices: 33.2 us -> 35.2 us
    ppermute x1, starting transfers between devices: 2.03 us -> 3.98 us  [shards(): other = lax.ppermute(own, 'v', swap)]
    all_to_all x1, blocking collectives: 23.6 us -> 22.3 us  [shards(): lax.all_to_all(partial, axes, split_axis=0, concat_axis=0, tiled=True, ax...]
where the time goes in v5:
time: 114 us; the launch traced here: 113 us
  blocking collectives  36.8 us (32%)
  starting transfers between devices  35.2 us (31%)
  waiting for transfers between devices  30.3 us (27%)
  Pallas kernels  5.87 us (5%)
  local copies, waits for them, and re-layouts  2.61 us (2%)
  other arithmetic  1.64 us (1%)
    all_to_all x1, blocking collectives, shards(): lax.all_to_all(partial, axes, split_axis=0, concat_axis=0, tiled=True, ax...  22.3 us
    all_gather x1, blocking collectives, shards(): own = lax.all_gather(mine, axes, axis=0, tiled=True, axis_index_groups=sets)  14.6 us
    ppermute x1, waiting for transfers between devices, shards(): near = lax.ppermute(near, 'v', swap)  13 us
    all_to_all x1, starting transfers between devices, shards(): lax.all_to_all(pieces, SEC, split_axis=0, concat_axis=0, tiled=True)  10.8 us
    all_to_all x1, starting transfers between devices, shards(): lax.all_to_all(chosen, SEC, split_axis=0, concat_axis=0, tiled=True)  10.1 us
    all_to_all x1, waiting for transfers between devices, shards(): lax.all_to_all(pieces, SEC, split_axis=0, concat_axis=0, tiled=True)  6.98 us
    ppermute x1, waiting for transfers between devices, shards(): other = lax.ppermute(own, 'v', swap)  6.65 us
    pallas_call x2, Pallas kernels, call(): pl.pallas_call(kernel, out_shape=jax.ShapeDtypeStruct(shape, jnp.bfloat16...  4.31 us
  transfers between devices with their start and end apart: 7, of which 5 were waited for; matrix products, arithmetic and copies ran while one was open for 2% of the time, Pallas kernels for 2%

profile of v5, /device:TPU:6, one launch (start us, length us, event | category | flops | bytes accessed | tf_op | source)
XLA Modules:
  0.0 113.3 jit_solution(17902301033881777278)
XLA Ops:
  0.6 0.0 copy-start.2
  0.6 0.0 copy-start.1
  0.7 1.1 broadcast_select_fusion
  1.8 1.2 %copy.16 = bf16[64,12,2,128]{3,2,1,0:T(2,128)(2,1)} copy(bf16[64,12,2,128]{3,0,2,1:T(8,128)(2,1)S(1)} %bitcast.11) | data formatting | bytes 786432 | tf_op jit(solution)/shard_map/transpose | solution.py:186
  2.9 10.8 %all-to-all-start = ((bf16[64,24,128]{2,1,0:T(8,128)(2,1)}), bf16[64,24,128]{2,1,0:T(8,128)(2,1)S(1)}, u32[]{:S(2)}, u32[]{:S(2)}) async-start(bf16[64,24,128]{2,1,0:T(8,128)(2,1)} %bitcast.2), calls=%async_computation | async-start | bytes 786432 | tf_op jit(solution)/shard_map/all_to_all | solution.py:188
  13.7 0.0 copy-done.2
  13.7 4.3 %collective-permute-start = (s32[1,768]{1,0:T(1,128)S(1)}, s32[1,768]{1,0:T(1,128)S(1)}, u32[]{:S(2)}, u32[]{:S(2)}) collective-permute-start(s32[1,768]{1,0:T(1,128)S(1)} %copy-done.2), channel_id=1, source_target_pairs={{0,64},{64,0},{1,65},{65,1},{2,66},{66,2},{3,67},{67,3},{4,68},{68... | collective-permute-start | bytes 9224 | tf_op jit(solution)/shard_map/ppermute | solution.py:184
  18.0 0.0 copy-done.1
  18.0 1.9 %collective-permute-start.1 = (bf16[5,2,128,128]{3,2,1,0:T(8,128)(2,1)S(1)}, bf16[5,2,128,128]{3,2,1,0:T(8,128)(2,1)S(1)}, u32[]{:S(2)}, u32[]{:S(2)}) collective-permute-start(bf16[5,2,128,128]{3,2,1,0:T(8,128)(2,1)S(1)} %copy-done.1), channel_id=1, source_target_pairs={{0,64},{64,0},{1,65},{65,1},{2,66},{66,2},{3,67},{67,3},{4,68},{68... | collective-permute-start | bytes 983048 | tf_op jit(solution)/shard_map/ppermute | solution.py:189
  20.0 0.1 stack_reshape.6
  20.1 0.0 collective-permute-done
  20.1 0.1 stack_reshape.7
  20.2 0.1 copy.17
  20.3 0.1 eq.19
  20.4 0.5 fusion.hot_ref
  20.9 7.0 %all-to-all-done = bf16[64,24,128]{2,1,0:T(8,128)(2,1)S(1)} async-done(((bf16[64,24,128]{2,1,0:T(8,128)(2,1)}), bf16[64,24,128]{2,1,0:T(8,128)(2,1)S(1)}, u32[]{:S(2)}, u32[]{:S(2)}) %all-to-all-start) | async-done | bytes 393248 | tf_op jit(solution)/shard_map/all_to_all | solution.py:188
  27.9 1.8 %choose.1 = bf16[1536,256]{1,0:T(8,128)(2,1)} custom-call(bf16[1536,128]{1,0:T(8,128)(2,1)S(1)} %bitcast.8, bf16[1536,768]{1,0:T(8,128)(2,1)S(1)} %fusion.hot_ref), custom_call_target="tpu_custom_call" | custom-call | flops 700000000 | bytes 4194304 | tf_op jit(solution)/shard_map/choose/pallas_call | solution.py:159
  29.6 0.0 copy-start
  29.7 0.0 collective-permute-done.1.left_b
  29.7 10.1 %all-to-all-start.1 = ((bf16[64,24,256]{2,1,0:T(8,128)(2,1)}), bf16[64,24,256]{2,1,0:T(8,128)(2,1)S(1)}, u32[]{:S(2)}, u32[]{:S(2)}) async-start(bf16[64,24,256]{2,1,0:T(8,128)(2,1)} %bitcast.4), calls=%async_computation.1 | async-start | bytes 1572864 | tf_op jit(solution)/shard_map/all_to_all | solution.py:207
  39.7 1.1 constant_dynamic-slice_fusion
  40.8 2.2 %collective-permute-start.2 = (bf16[5,3,128,128]{3,2,1,0:T(8,128)(2,1)S(1)}, bf16[5,3,128,128]{3,2,1,0:T(8,128)(2,1)S(1)}, u32[]{:S(2)}, u32[]{:S(2)}) collective-permute-start(bf16[5,3,128,128]{3,2,1,0:T(8,128)(2,1)S(1)} %constant_dynamic-slice_fusion), channel_id=1, source_target_pairs={{0,64},{64,0},{1,65},{65,1},{2,66},{66,2},{3,67},{67,3},{4,68},{68... | collective-permute-start | bytes 1474568 | tf_op jit(solution)/shard_map/ppermute | solution.py:209
  43.0 13.0 %collective-permute-done.2.near_ref = bf16[5,3,128,128]{3,2,1,0:T(8,128)(2,1)S(1)} collective-permute-done((bf16[5,3,128,128]{3,2,1,0:T(8,128)(2,1)S(1)}, bf16[5,3,128,128]{3,2,1,0:T(8,128)(2,1)S(1)}, u32[]{:S(2)}, u32[]{:S(2)}) %collective-permute-start.2) | collective-permute-done | bytes 491552 | tf_op jit(solution)/shard_map/ppermute | solution.py:209
  56.0 1.9 %collective-permute-start.3 = (bf16[5,3,128,128]{3,2,1,0:T(8,128)(2,1)S(1)}, bf16[5,3,128,128]{3,2,1,0:T(8,128)(2,1)S(1)}, u32[]{:S(2)}, u32[]{:S(2)}) collective-permute-start(bf16[5,3,128,128]{3,2,1,0:T(8,128)(2,1)S(1)} %collective-permute-done.2.near_ref), channel_id=1, source_target_pairs={{0,1},{1,0},{2,3},{3,2},{4,5},{5,4},{6,7},{7,6},{8,9},{9,8},{10,11... | collective-permute-start | bytes 1474568 | tf_op jit(solution)/shard_map/ppermute | solution.py:210
  57.9 1.8 %collective-permute-done.3.far_ref = bf16[5,3,128,128]{3,2,1,0:T(8,128)(2,1)S(1)} collective-permute-done((bf16[5,3,128,128]{3,2,1,0:T(8,128)(2,1)S(1)}, bf16[5,3,128,128]{3,2,1,0:T(8,128)(2,1)S(1)}, u32[]{:S(2)}, u32[]{:S(2)}) %collective-permute-start.3) | collective-permute-done | bytes 491552 | tf_op jit(solution)/shard_map/ppermute | solution.py:210
  59.7 1.9 %all-to-all-done.1 = bf16[64,24,256]{2,1,0:T(8,128)(2,1)S(1)} async-done(((bf16[64,24,256]{2,1,0:T(8,128)(2,1)}), bf16[64,24,256]{2,1,0:T(8,128)(2,1)S(1)}, u32[]{:S(2)}, u32[]{:S(2)}) %all-to-all-start.1) | async-done | bytes 786464 | tf_op jit(solution)/shard_map/all_to_all | solution.py:207
  61.6 0.0 copy-done
  61.6 2.5 %apply.1 = bf16[12,128,128]{2,1,0:T(8,128)(2,1)S(1)} custom-call(bf16[1536,256]{1,0:T(8,128)(2,1)S(1)} %bitcast.9, bf16[5,2,128,128]{3,2,1,0:T(8,128)(2,1)S(1)} %copy-done.1, bf16[5,2,128,128]{3,2,1,0:T(8,128)(2,1)S(1)} %collective-permute-done.1.left_b, bf16[5,6,128,128]{3,2,1,0:T(8,128)(2,1)S(1)} %copy-done, ...), custom_call_target="tpu_custom_call" | custom-call | flops 2000000000 | bytes 4194304 | tf_op jit(solution)/shard_map/apply/pallas_call | solution.py:159
  64.2 22.3 %all_to_all.27 = bf16[12,128,128]{2,1,0:T(8,128)(2,1)S(1)} all-to-all(bf16[12,128,128]{2,1,0:T(8,128)(2,1)S(1)} %apply.1), channel_id=1, replica_groups={{0,128,256,384},{385,257,129,1},{64,192,320,448},{449,321,193,65},{2,13..., dimensions={0} | all-to-all | bytes 786432 | tf_op jit(solution)/shard_map/all_to_all | solution.py:230
  86.5 0.1 reduce_sum.12
  86.5 14.6 %all_gather.3.data_ref = bf16[12,128,128]{2,1,0:T(8,128)(2,1)S(1)} all-gather(bf16[3,128,128]{2,1,0:T(8,128)(2,1)S(1)} %reduce_sum.12), channel_id=1, replica_groups={{0,128,256,384},{385,257,129,1},{64,192,320,448},{449,321,193,65},{2,13..., dimensions={0}, use_global_device_ids=true | all-gather | bytes 491520 | tf_op jit(solution)/shard_map/all_gather | solution.py:235
  101.1 4.0 %collective-permute-start.4 = (bf16[12,128,128]{2,1,0:T(8,128)(2,1)S(1)}, bf16[12,128,128]{2,1,0:T(8,128)(2,1)S(1)}, u32[]{:S(2)}, u32[]{:S(2)}) collective-permute-start(bf16[12,128,128]{2,1,0:T(8,128)(2,1)S(1)} %all_gather.3.data_ref), channel_id=1, source_target_pairs={{0,64},{64,0},{1,65},{65,1},{2,66},{66,2},{3,67},{67,3},{4,68},{68... | collective-permute-start | bytes 1179656 | tf_op jit(solution)/shard_map/ppermute | solution.py:236
  105.1 0.8 place.2
  105.9 6.7 %collective-permute-done.4.data_ref = bf16[12,128,128]{2,1,0:T(8,128)(2,1)S(1)} collective-permute-done((bf16[12,128,128]{2,1,0:T(8,128)(2,1)S(1)}, bf16[12,128,128]{2,1,0:T(8,128)(2,1)S(1)}, u32[]{:S(2)}, u32[]{:S(2)}) %collective-permute-start.4) | collective-permute-done | bytes 393248 | tf_op jit(solution)/shard_map/ppermute | solution.py:236
  112.5 0.8 place.3
  (3 shorter events, 0.0 us)
Async XLA Ops:
  0.6 13.1 %copy-start.2 = (s32[1,768]{1,0:T(1,128)S(1)}, s32[1,768]{1,0:T(1,128)}, u32[]{:S(2)}) copy-start(s32[1,768]{1,0:T(1,128)} %param.9) | copy-start | bytes 9220
  0.6 17.4 %copy-start.1 = (bf16[5,2,128,128]{3,2,1,0:T(8,128)(2,1)S(1)}, bf16[5,2,128,128]{3,2,1,0:T(8,128)(2,1)}, u32[]{:S(2)}) copy-start(bf16[5,2,128,128]{3,2,1,0:T(8,128)(2,1)} %left_a.1) | copy-start | bytes 983044
  2.9 25.0 %all-to-all-start = ((bf16[64,24,128]{2,1,0:T(8,128)(2,1)}), bf16[64,24,128]{2,1,0:T(8,128)(2,1)S(1)}, u32[]{:S(2)}, u32[]{:S(2)}) async-start(bf16[64,24,128]{2,1,0:T(8,128)(2,1)} %bitcast.2), calls=%async_computation | async-start | bytes 786432 | tf_op jit(solution)/shard_map/all_to_all | solution.py:188
  13.7 6.4 %collective-permute-start = (s32[1,768]{1,0:T(1,128)S(1)}, s32[1,768]{1,0:T(1,128)S(1)}, u32[]{:S(2)}, u32[]{:S(2)}) collective-permute-start(s32[1,768]{1,0:T(1,128)S(1)} %copy-done.2), channel_id=1, source_target_pairs={{0,64},{64,0},{1,65},{65,1},{2,66},{66,2},{3,67},{67,3},{4,68},{68... | collective-permute-start | bytes 9224 | tf_op jit(solution)/shard_map/ppermute | solution.py:184
  18.0 11.6 %collective-permute-start.1 = (bf16[5,2,128,128]{3,2,1,0:T(8,128)(2,1)S(1)}, bf16[5,2,128,128]{3,2,1,0:T(8,128)(2,1)S(1)}, u32[]{:S(2)}, u32[]{:S(2)}) collective-permute-start(bf16[5,2,128,128]{3,2,1,0:T(8,128)(2,1)S(1)} %copy-done.1), channel_id=1, source_target_pairs={{0,64},{64,0},{1,65},{65,1},{2,66},{66,2},{3,67},{67,3},{4,68},{68... | collective-permute-start | bytes 983048 | tf_op jit(solution)/shard_map/ppermute | solution.py:189
  29.6 32.0 %copy-start = (bf16[5,6,128,128]{3,2,1,0:T(8,128)(2,1)S(1)}, bf16[5,6,128,128]{3,2,1,0:T(8,128)(2,1)}, u32[]{:S(2)}) copy-start(bf16[5,6,128,128]{3,2,1,0:T(8,128)(2,1)} %right_a.1) | copy-start | bytes 2949124
  29.7 32.0 %all-to-all-start.1 = ((bf16[64,24,256]{2,1,0:T(8,128)(2,1)}), bf16[64,24,256]{2,1,0:T(8,128)(2,1)S(1)}, u32[]{:S(2)}, u32[]{:S(2)}) async-start(bf16[64,24,256]{2,1,0:T(8,128)(2,1)} %bitcast.4), calls=%async_computation.1 | async-start | bytes 1572864 | tf_op jit(solution)/shard_map/all_to_all | solution.py:207
  40.8 15.2 %collective-permute-start.2 = (bf16[5,3,128,128]{3,2,1,0:T(8,128)(2,1)S(1)}, bf16[5,3,128,128]{3,2,1,0:T(8,128)(2,1)S(1)}, u32[]{:S(2)}, u32[]{:S(2)}) collective-permute-start(bf16[5,3,128,128]{3,2,1,0:T(8,128)(2,1)S(1)} %constant_dynamic-slice_fusion), channel_id=1, source_target_pairs={{0,64},{64,0},{1,65},{65,1},{2,66},{66,2},{3,67},{67,3},{4,68},{68... | collective-permute-start | bytes 1474568 | tf_op jit(solution)/shard_map/ppermute | solution.py:209
  56.0 3.7 %collective-permute-start.3 = (bf16[5,3,128,128]{3,2,1,0:T(8,128)(2,1)S(1)}, bf16[5,3,128,128]{3,2,1,0:T(8,128)(2,1)S(1)}, u32[]{:S(2)}, u32[]{:S(2)}) collective-permute-start(bf16[5,3,128,128]{3,2,1,0:T(8,128)(2,1)S(1)} %collective-permute-done.2.near_ref), channel_id=1, source_target_pairs={{0,1},{1,0},{2,3},{3,2},{4,5},{5,4},{6,7},{7,6},{8,9},{9,8},{10,11... | collective-permute-start | bytes 1474568 | tf_op jit(solution)/shard_map/ppermute | solution.py:210
  101.1 11.4 %collective-permute-start.4 = (bf16[12,128,128]{2,1,0:T(8,128)(2,1)S(1)}, bf16[12,128,128]{2,1,0:T(8,128)(2,1)S(1)}, u32[]{:S(2)}, u32[]{:S(2)}) collective-permute-start(bf16[12,128,128]{2,1,0:T(8,128)(2,1)S(1)} %all_gather.3.data_ref), channel_id=1, source_target_pairs={{0,64},{64,0},{1,65},{65,1},{2,66},{66,2},{3,67},{67,3},{4,68},{68... | collective-permute-start | bytes 1179656 | tf_op jit(solution)/shard_map/ppermute | solution.py:236

commit v6 on v5

--- a/solution.py
+++ b/solution.py
@@ -223,7 +223,7 @@
     quarters = lax.axis_size("q")
     axes = ("q", "v", "core")
     sets = [
-        [(q * 2 + v) * 2 + c for q in (range(quarters) if c == 0 else reversed(range(quarters)))]
+        [(q * 2 + v) * 2 + c for q in (range(quarters) if c == 1 else reversed(range(quarters)))]
         for v in range(2)
         for c in range(2)
     ]

time: 114 us -> 114 us (level)
  no operation moved by 1% of the time
where the time goes in v6:
time: 114 us; the launch traced here: 113 us
  blocking collectives  36.8 us (32%)
  starting transfers between devices  34.5 us (30%)
  waiting for transfers between devices  30.8 us (27%)
  Pallas kernels  5.87 us (5%)
  local copies, waits for them, and re-layouts  2.61 us (2%)
  other arithmetic  1.64 us (1%)
    all_to_all x1, blocking collectives, shards(): lax.all_to_all(partial, axes, split_axis=0, concat_axis=0, tiled=True, ax...  21.7 us
    all_gather x1, blocking collectives, shards(): own = lax.all_gather(mine, axes, axis=0, tiled=True, axis_index_groups=sets)  15 us
    ppermute x1, waiting for transfers between devices, shards(): near = lax.ppermute(near, 'v', swap)  13 us
    all_to_all x1, starting transfers between devices, shards(): lax.all_to_all(pieces, SEC, split_axis=0, concat_axis=0, tiled=True)  10.8 us
    all_to_all x1, starting transfers between devices, shards(): lax.all_to_all(chosen, SEC, split_axis=0, concat_axis=0, tiled=True)  10.1 us
    ppermute x1, waiting for transfers between devices, shards(): other = lax.ppermute(own, 'v', swap)  7.13 us
    all_to_all x1, waiting for transfers between devices, shards(): lax.all_to_all(pieces, SEC, split_axis=0, concat_axis=0, tiled=True)  6.98 us
    pallas_call x2, Pallas kernels, call(): pl.pallas_call(kernel, out_shape=jax.ShapeDtypeStruct(shape, jnp.bfloat16...  4.31 us
  transfers between devices with their start and end apart: 7, of which 5 were waited for; matrix products, arithmetic and copies ran while one was open for 2% of the time, Pallas kernels for 2%

profile of v6, /device:TPU:6, one launch (start us, length us, event | category | flops | bytes accessed | tf_op | source)
XLA Modules:
  0.0 113.1 jit_solution(13475563056345707469)
XLA Ops:
  0.6 0.0 copy-start.2
  0.6 0.0 copy-start.1
  0.7 1.1 broadcast_select_fusion
  1.8 1.2 %copy.16 = bf16[64,12,2,128]{3,2,1,0:T(2,128)(2,1)} copy(bf16[64,12,2,128]{3,0,2,1:T(8,128)(2,1)S(1)} %bitcast.11) | data formatting | bytes 786432 | tf_op jit(solution)/shard_map/transpose | solution.py:186
  2.9 10.8 %all-to-all-start = ((bf16[64,24,128]{2,1,0:T(8,128)(2,1)}), bf16[64,24,128]{2,1,0:T(8,128)(2,1)S(1)}, u32[]{:S(2)}, u32[]{:S(2)}) async-start(bf16[64,24,128]{2,1,0:T(8,128)(2,1)} %bitcast.2), calls=%async_computation | async-start | bytes 786432 | tf_op jit(solution)/shard_map/all_to_all | solution.py:188
  13.7 0.0 copy-done.2
  13.7 4.3 %collective-permute-start = (s32[1,768]{1,0:T(1,128)S(1)}, s32[1,768]{1,0:T(1,128)S(1)}, u32[]{:S(2)}, u32[]{:S(2)}) collective-permute-start(s32[1,768]{1,0:T(1,128)S(1)} %copy-done.2), channel_id=1, source_target_pairs={{0,64},{64,0},{1,65},{65,1},{2,66},{66,2},{3,67},{67,3},{4,68},{68... | collective-permute-start | bytes 9224 | tf_op jit(solution)/shard_map/ppermute | solution.py:184
  18.0 0.0 copy-done.1
  18.0 1.9 %collective-permute-start.1 = (bf16[5,2,128,128]{3,2,1,0:T(8,128)(2,1)S(1)}, bf16[5,2,128,128]{3,2,1,0:T(8,128)(2,1)S(1)}, u32[]{:S(2)}, u32[]{:S(2)}) collective-permute-start(bf16[5,2,128,128]{3,2,1,0:T(8,128)(2,1)S(1)} %copy-done.1), channel_id=1, source_target_pairs={{0,64},{64,0},{1,65},{65,1},{2,66},{66,2},{3,67},{67,3},{4,68},{68... | collective-permute-start | bytes 983048 | tf_op jit(solution)/shard_map/ppermute | solution.py:189
  20.0 0.1 stack_reshape.6
  20.1 0.0 collective-permute-done
  20.1 0.1 stack_reshape.7
  20.2 0.1 copy.17
  20.3 0.1 eq.19
  20.4 0.5 fusion.hot_ref
  20.9 7.0 %all-to-all-done = bf16[64,24,128]{2,1,0:T(8,128)(2,1)S(1)} async-done(((bf16[64,24,128]{2,1,0:T(8,128)(2,1)}), bf16[64,24,128]{2,1,0:T(8,128)(2,1)S(1)}, u32[]{:S(2)}, u32[]{:S(2)}) %all-to-all-start) | async-done | bytes 393248 | tf_op jit(solution)/shard_map/all_to_all | solution.py:188
  27.9 1.8 %choose.1 = bf16[1536,256]{1,0:T(8,128)(2,1)} custom-call(bf16[1536,128]{1,0:T(8,128)(2,1)S(1)} %bitcast.8, bf16[1536,768]{1,0:T(8,128)(2,1)S(1)} %fusion.hot_ref), custom_call_target="tpu_custom_call" | custom-call | flops 700000000 | bytes 4194304 | tf_op jit(solution)/shard_map/choose/pallas_call | solution.py:159
  29.6 0.0 copy-start
  29.7 0.0 collective-permute-done.1.left_b
  29.7 10.1 %all-to-all-start.1 = ((bf16[64,24,256]{2,1,0:T(8,128)(2,1)}), bf16[64,24,256]{2,1,0:T(8,128)(2,1)S(1)}, u32[]{:S(2)}, u32[]{:S(2)}) async-start(bf16[64,24,256]{2,1,0:T(8,128)(2,1)} %bitcast.4), calls=%async_computation.1 | async-start | bytes 1572864 | tf_op jit(solution)/shard_map/all_to_all | solution.py:207
  39.7 1.1 constant_dynamic-slice_fusion
  40.8 2.2 %collective-permute-start.2 = (bf16[5,3,128,128]{3,2,1,0:T(8,128)(2,1)S(1)}, bf16[5,3,128,128]{3,2,1,0:T(8,128)(2,1)S(1)}, u32[]{:S(2)}, u32[]{:S(2)}) collective-permute-start(bf16[5,3,128,128]{3,2,1,0:T(8,128)(2,1)S(1)} %constant_dynamic-slice_fusion), channel_id=1, source_target_pairs={{0,64},{64,0},{1,65},{65,1},{2,66},{66,2},{3,67},{67,3},{4,68},{68... | collective-permute-start | bytes 1474568 | tf_op jit(solution)/shard_map/ppermute | solution.py:209
  43.0 13.0 %collective-permute-done.2.near_ref = bf16[5,3,128,128]{3,2,1,0:T(8,128)(2,1)S(1)} collective-permute-done((bf16[5,3,128,128]{3,2,1,0:T(8,128)(2,1)S(1)}, bf16[5,3,128,128]{3,2,1,0:T(8,128)(2,1)S(1)}, u32[]{:S(2)}, u32[]{:S(2)}) %collective-permute-start.2) | collective-permute-done | bytes 491552 | tf_op jit(solution)/shard_map/ppermute | solution.py:209
  56.0 1.9 %collective-permute-start.3 = (bf16[5,3,128,128]{3,2,1,0:T(8,128)(2,1)S(1)}, bf16[5,3,128,128]{3,2,1,0:T(8,128)(2,1)S(1)}, u32[]{:S(2)}, u32[]{:S(2)}) collective-permute-start(bf16[5,3,128,128]{3,2,1,0:T(8,128)(2,1)S(1)} %collective-permute-done.2.near_ref), channel_id=1, source_target_pairs={{0,1},{1,0},{2,3},{3,2},{4,5},{5,4},{6,7},{7,6},{8,9},{9,8},{10,11... | collective-permute-start | bytes 1474568 | tf_op jit(solution)/shard_map/ppermute | solution.py:210
  57.9 1.8 %collective-permute-done.3.far_ref = bf16[5,3,128,128]{3,2,1,0:T(8,128)(2,1)S(1)} collective-permute-done((bf16[5,3,128,128]{3,2,1,0:T(8,128)(2,1)S(1)}, bf16[5,3,128,128]{3,2,1,0:T(8,128)(2,1)S(1)}, u32[]{:S(2)}, u32[]{:S(2)}) %collective-permute-start.3) | collective-permute-done | bytes 491552 | tf_op jit(solution)/shard_map/ppermute | solution.py:210
  59.7 1.9 %all-to-all-done.1 = bf16[64,24,256]{2,1,0:T(8,128)(2,1)S(1)} async-done(((bf16[64,24,256]{2,1,0:T(8,128)(2,1)}), bf16[64,24,256]{2,1,0:T(8,128)(2,1)S(1)}, u32[]{:S(2)}, u32[]{:S(2)}) %all-to-all-start.1) | async-done | bytes 786464 | tf_op jit(solution)/shard_map/all_to_all | solution.py:207
  61.6 0.0 copy-done
  61.6 2.5 %apply.1 = bf16[12,128,128]{2,1,0:T(8,128)(2,1)S(1)} custom-call(bf16[1536,256]{1,0:T(8,128)(2,1)S(1)} %bitcast.9, bf16[5,2,128,128]{3,2,1,0:T(8,128)(2,1)S(1)} %copy-done.1, bf16[5,2,128,128]{3,2,1,0:T(8,128)(2,1)S(1)} %collective-permute-done.1.left_b, bf16[5,6,128,128]{3,2,1,0:T(8,128)(2,1)S(1)} %copy-done, ...), custom_call_target="tpu_custom_call" | custom-call | flops 2000000000 | bytes 4194304 | tf_op jit(solution)/shard_map/apply/pallas_call | solution.py:159
  64.2 21.7 %all_to_all.27 = bf16[12,128,128]{2,1,0:T(8,128)(2,1)S(1)} all-to-all(bf16[12,128,128]{2,1,0:T(8,128)(2,1)S(1)} %apply.1), channel_id=1, replica_groups={{384,256,128,0},{1,129,257,385},{448,320,192,64},{65,193,321,449},{386,..., dimensions={0} | all-to-all | bytes 786432 | tf_op jit(solution)/shard_map/all_to_all | solution.py:230
  85.9 0.1 reduce_sum.12
  86.0 15.0 %all_gather.3.data_ref = bf16[12,128,128]{2,1,0:T(8,128)(2,1)S(1)} all-gather(bf16[3,128,128]{2,1,0:T(8,128)(2,1)S(1)} %reduce_sum.12), channel_id=1, replica_groups={{384,256,128,0},{1,129,257,385},{448,320,192,64},{65,193,321,449},{386,..., dimensions={0}, use_global_device_ids=true | all-gather | bytes 491520 | tf_op jit(solution)/shard_map/all_gather | solution.py:235
  101.0 3.3 %collective-permute-start.4 = (bf16[12,128,128]{2,1,0:T(8,128)(2,1)S(1)}, bf16[12,128,128]{2,1,0:T(8,128)(2,1)S(1)}, u32[]{:S(2)}, u32[]{:S(2)}) collective-permute-start(bf16[12,128,128]{2,1,0:T(8,128)(2,1)S(1)} %all_gather.3.data_ref), channel_id=1, source_target_pairs={{0,64},{64,0},{1,65},{65,1},{2,66},{66,2},{3,67},{67,3},{4,68},{68... | collective-permute-start | bytes 1179656 | tf_op jit(solution)/shard_map/ppermute | solution.py:236
  104.4 0.8 place.2
  105.2 7.1 %collective-permute-done.4.data_ref = bf16[12,128,128]{2,1,0:T(8,128)(2,1)S(1)} collective-permute-done((bf16[12,128,128]{2,1,0:T(8,128)(2,1)S(1)}, bf16[12,128,128]{2,1,0:T(8,128)(2,1)S(1)}, u32[]{:S(2)}, u32[]{:S(2)}) %collective-permute-start.4) | collective-permute-done | bytes 393248 | tf_op jit(solution)/shard_map/ppermute | solution.py:236
  112.3 0.8 place.3
  (3 shorter events, 0.0 us)
Async XLA Ops:
  0.6 13.1 %copy-start.2 = (s32[1,768]{1,0:T(1,128)S(1)}, s32[1,768]{1,0:T(1,128)}, u32[]{:S(2)}) copy-start(s32[1,768]{1,0:T(1,128)} %param.9) | copy-start | bytes 9220
  0.6 17.4 %copy-start.1 = (bf16[5,2,128,128]{3,2,1,0:T(8,128)(2,1)S(1)}, bf16[5,2,128,128]{3,2,1,0:T(8,128)(2,1)}, u32[]{:S(2)}) copy-start(bf16[5,2,128,128]{3,2,1,0:T(8,128)(2,1)} %left_a.1) | copy-start | bytes 983044
  2.9 25.0 %all-to-all-start = ((bf16[64,24,128]{2,1,0:T(8,128)(2,1)}), bf16[64,24,128]{2,1,0:T(8,128)(2,1)S(1)}, u32[]{:S(2)}, u32[]{:S(2)}) async-start(bf16[64,24,128]{2,1,0:T(8,128)(2,1)} %bitcast.2), calls=%async_computation | async-start | bytes 786432 | tf_op jit(solution)/shard_map/all_to_all | solution.py:188
  13.7 6.4 %collective-permute-start = (s32[1,768]{1,0:T(1,128)S(1)}, s32[1,768]{1,0:T(1,128)S(1)}, u32[]{:S(2)}, u32[]{:S(2)}) collective-permute-start(s32[1,768]{1,0:T(1,128)S(1)} %copy-done.2), channel_id=1, source_target_pairs={{0,64},{64,0},{1,65},{65,1},{2,66},{66,2},{3,67},{67,3},{4,68},{68... | collective-permute-start | bytes 9224 | tf_op jit(solution)/shard_map/ppermute | solution.py:184
  18.0 11.6 %collective-permute-start.1 = (bf16[5,2,128,128]{3,2,1,0:T(8,128)(2,1)S(1)}, bf16[5,2,128,128]{3,2,1,0:T(8,128)(2,1)S(1)}, u32[]{:S(2)}, u32[]{:S(2)}) collective-permute-start(bf16[5,2,128,128]{3,2,1,0:T(8,128)(2,1)S(1)} %copy-done.1), channel_id=1, source_target_pairs={{0,64},{64,0},{1,65},{65,1},{2,66},{66,2},{3,67},{67,3},{4,68},{68... | collective-permute-start | bytes 983048 | tf_op jit(solution)/shard_map/ppermute | solution.py:189
  29.6 32.0 %copy-start = (bf16[5,6,128,128]{3,2,1,0:T(8,128)(2,1)S(1)}, bf16[5,6,128,128]{3,2,1,0:T(8,128)(2,1)}, u32[]{:S(2)}) copy-start(bf16[5,6,128,128]{3,2,1,0:T(8,128)(2,1)} %right_a.1) | copy-start | bytes 2949124
  29.7 32.0 %all-to-all-start.1 = ((bf16[64,24,256]{2,1,0:T(8,128)(2,1)}), bf16[64,24,256]{2,1,0:T(8,128)(2,1)S(1)}, u32[]{:S(2)}, u32[]{:S(2)}) async-start(bf16[64,24,256]{2,1,0:T(8,128)(2,1)} %bitcast.4), calls=%async_computation.1 | async-start | bytes 1572864 | tf_op jit(solution)/shard_map/all_to_all | solution.py:207
  40.8 15.2 %collective-permute-start.2 = (bf16[5,3,128,128]{3,2,1,0:T(8,128)(2,1)S(1)}, bf16[5,3,128,128]{3,2,1,0:T(8,128)(2,1)S(1)}, u32[]{:S(2)}, u32[]{:S(2)}) collective-permute-start(bf16[5,3,128,128]{3,2,1,0:T(8,128)(2,1)S(1)} %constant_dynamic-slice_fusion), channel_id=1, source_target_pairs={{0,64},{64,0},{1,65},{65,1},{2,66},{66,2},{3,67},{67,3},{4,68},{68... | collective-permute-start | bytes 1474568 | tf_op jit(solution)/shard_map/ppermute | solution.py:209
  56.0 3.7 %collective-permute-start.3 = (bf16[5,3,128,128]{3,2,1,0:T(8,128)(2,1)S(1)}, bf16[5,3,128,128]{3,2,1,0:T(8,128)(2,1)S(1)}, u32[]{:S(2)}, u32[]{:S(2)}) collective-permute-start(bf16[5,3,128,128]{3,2,1,0:T(8,128)(2,1)S(1)} %collective-permute-done.2.near_ref), channel_id=1, source_target_pairs={{0,1},{1,0},{2,3},{3,2},{4,5},{5,4},{6,7},{7,6},{8,9},{9,8},{10,11... | collective-permute-start | bytes 1474568 | tf_op jit(solution)/shard_map/ppermute | solution.py:210
  101.0 11.3 %collective-permute-start.4 = (bf16[12,128,128]{2,1,0:T(8,128)(2,1)S(1)}, bf16[12,128,128]{2,1,0:T(8,128)(2,1)S(1)}, u32[]{:S(2)}, u32[]{:S(2)}) collective-permute-start(bf16[12,128,128]{2,1,0:T(8,128)(2,1)S(1)} %all_gather.3.data_ref), channel_id=1, source_target_pairs={{0,64},{64,0},{1,65},{65,1},{2,66},{66,2},{3,67},{67,3},{4,68},{68... | collective-permute-start | bytes 1179656 | tf_op jit(solution)/shard_map/ppermute | solution.py:236

commit v7 on v5

--- a/solution.py
+++ b/solution.py
@@ -9,7 +9,7 @@
 
 VMEM_LIMIT = 30 * 1024 * 1024
 SLAB = 16
-STEPS = 6
+STEPS = 12
 SEC = ("chip", "core")
 
 

time: 114 us -> 114 us (level)
  no operation moved by 1% of the time
where the time goes in v7:
time: 114 us; the launch traced here: 113 us
  blocking collectives  36.8 us (32%)
  starting transfers between devices  35.1 us (31%)
  waiting for transfers between devices  30.3 us (27%)
  Pallas kernels  5.96 us (5%)
  local copies, waits for them, and re-layouts  2.61 us (2%)
  other arithmetic  1.64 us (1%)
    all_to_all x1, blocking collectives, shards(): lax.all_to_all(partial, axes, split_axis=0, concat_axis=0, tiled=True, ax...  22.3 us
    all_gather x1, blocking collectives, shards(): own = lax.all_gather(mine, axes, axis=0, tiled=True, axis_index_groups=sets)  14.6 us
    ppermute x1, waiting for transfers between devices, shards(): near = lax.ppermute(near, 'v', swap)  13 us
    all_to_all x1, starting transfers between devices, shards(): lax.all_to_all(pieces, SEC, split_axis=0, concat_axis=0, tiled=True)  10.8 us
    all_to_all x1, starting transfers between devices, shards(): lax.all_to_all(chosen, SEC, split_axis=0, concat_axis=0, tiled=True)  9.97 us
    all_to_all x1, waiting for transfers between devices, shards(): lax.all_to_all(pieces, SEC, split_axis=0, concat_axis=0, tiled=True)  6.98 us
    ppermute x1, waiting for transfers between devices, shards(): other = lax.ppermute(own, 'v', swap)  6.65 us
    pallas_call x2, Pallas kernels, call(): pl.pallas_call(kernel, out_shape=jax.ShapeDtypeStruct(shape, jnp.bfloat16...  4.4 us
  transfers between devices with their start and end apart: 7, of which 5 were waited for; matrix products, arithmetic and copies ran while one was open for 2% of the time, Pallas kernels for 2%

profile of v7, /device:TPU:6, one launch (start us, length us, event | category | flops | bytes accessed | tf_op | source)
XLA Modules:
  0.0 113.3 jit_solution(4565936861561269258)
XLA Ops:
  0.6 0.0 copy-start.2
  0.6 0.0 copy-start.1
  0.7 1.1 broadcast_select_fusion
  1.8 1.2 %copy.16 = bf16[64,12,2,128]{3,2,1,0:T(2,128)(2,1)} copy(bf16[64,12,2,128]{3,0,2,1:T(8,128)(2,1)S(1)} %bitcast.11) | data formatting | bytes 786432 | tf_op jit(solution)/shard_map/transpose | solution.py:186
  2.9 10.8 %all-to-all-start = ((bf16[64,24,128]{2,1,0:T(8,128)(2,1)}), bf16[64,24,128]{2,1,0:T(8,128)(2,1)S(1)}, u32[]{:S(2)}, u32[]{:S(2)}) async-start(bf16[64,24,128]{2,1,0:T(8,128)(2,1)} %bitcast.2), calls=%async_computation | async-start | bytes 786432 | tf_op jit(solution)/shard_map/all_to_all | solution.py:188
  13.7 0.0 copy-done.2
  13.7 4.3 %collective-permute-start = (s32[1,768]{1,0:T(1,128)S(1)}, s32[1,768]{1,0:T(1,128)S(1)}, u32[]{:S(2)}, u32[]{:S(2)}) collective-permute-start(s32[1,768]{1,0:T(1,128)S(1)} %copy-done.2), channel_id=1, source_target_pairs={{0,64},{64,0},{1,65},{65,1},{2,66},{66,2},{3,67},{67,3},{4,68},{68... | collective-permute-start | bytes 9224 | tf_op jit(solution)/shard_map/ppermute | solution.py:184
  18.0 0.0 copy-done.1
  18.0 1.9 %collective-permute-start.1 = (bf16[5,2,128,128]{3,2,1,0:T(8,128)(2,1)S(1)}, bf16[5,2,128,128]{3,2,1,0:T(8,128)(2,1)S(1)}, u32[]{:S(2)}, u32[]{:S(2)}) collective-permute-start(bf16[5,2,128,128]{3,2,1,0:T(8,128)(2,1)S(1)} %copy-done.1), channel_id=1, source_target_pairs={{0,64},{64,0},{1,65},{65,1},{2,66},{66,2},{3,67},{67,3},{4,68},{68... | collective-permute-start | bytes 983048 | tf_op jit(solution)/shard_map/ppermute | solution.py:189
  20.0 0.1 stack_reshape.6
  20.1 0.0 collective-permute-done
  20.1 0.1 stack_reshape.7
  20.2 0.1 copy.17
  20.3 0.1 eq.19
  20.4 0.5 fusion.hot_ref
  20.9 7.0 %all-to-all-done = bf16[64,24,128]{2,1,0:T(8,128)(2,1)S(1)} async-done(((bf16[64,24,128]{2,1,0:T(8,128)(2,1)}), bf16[64,24,128]{2,1,0:T(8,128)(2,1)S(1)}, u32[]{:S(2)}, u32[]{:S(2)}) %all-to-all-start) | async-done | bytes 393248 | tf_op jit(solution)/shard_map/all_to_all | solution.py:188
  27.9 1.9 %choose.1 = bf16[1536,256]{1,0:T(8,128)(2,1)} custom-call(bf16[1536,128]{1,0:T(8,128)(2,1)S(1)} %bitcast.8, bf16[1536,768]{1,0:T(8,128)(2,1)S(1)} %fusion.hot_ref), custom_call_target="tpu_custom_call" | custom-call | flops 700000000 | bytes 4194304 | tf_op jit(solution)/shard_map/choose/pallas_call | solution.py:159
  29.7 0.0 copy-start
  29.7 0.0 collective-permute-done.1.left_b
  29.8 10.0 %all-to-all-start.1 = ((bf16[64,24,256]{2,1,0:T(8,128)(2,1)}), bf16[64,24,256]{2,1,0:T(8,128)(2,1)S(1)}, u32[]{:S(2)}, u32[]{:S(2)}) async-start(bf16[64,24,256]{2,1,0:T(8,128)(2,1)} %bitcast.4), calls=%async_computation.1 | async-start | bytes 1572864 | tf_op jit(solution)/shard_map/all_to_all | solution.py:207
  39.7 1.1 constant_dynamic-slice_fusion
  40.8 2.2 %collective-permute-start.2 = (bf16[5,3,128,128]{3,2,1,0:T(8,128)(2,1)S(1)}, bf16[5,3,128,128]{3,2,1,0:T(8,128)(2,1)S(1)}, u32[]{:S(2)}, u32[]{:S(2)}) collective-permute-start(bf16[5,3,128,128]{3,2,1,0:T(8,128)(2,1)S(1)} %constant_dynamic-slice_fusion), channel_id=1, source_target_pairs={{0,64},{64,0},{1,65},{65,1},{2,66},{66,2},{3,67},{67,3},{4,68},{68... | collective-permute-start | bytes 1474568 | tf_op jit(solution)/shard_map/ppermute | solution.py:209
  43.0 13.0 %collective-permute-done.2.near_ref = bf16[5,3,128,128]{3,2,1,0:T(8,128)(2,1)S(1)} collective-permute-done((bf16[5,3,128,128]{3,2,1,0:T(8,128)(2,1)S(1)}, bf16[5,3,128,128]{3,2,1,0:T(8,128)(2,1)S(1)}, u32[]{:S(2)}, u32[]{:S(2)}) %collective-permute-start.2) | collective-permute-done | bytes 491552 | tf_op jit(solution)/shard_map/ppermute | solution.py:209
  56.0 1.9 %collective-permute-start.3 = (bf16[5,3,128,128]{3,2,1,0:T(8,128)(2,1)S(1)}, bf16[5,3,128,128]{3,2,1,0:T(8,128)(2,1)S(1)}, u32[]{:S(2)}, u32[]{:S(2)}) collective-permute-start(bf16[5,3,128,128]{3,2,1,0:T(8,128)(2,1)S(1)} %collective-permute-done.2.near_ref), channel_id=1, source_target_pairs={{0,1},{1,0},{2,3},{3,2},{4,5},{5,4},{6,7},{7,6},{8,9},{9,8},{10,11... | collective-permute-start | bytes 1474568 | tf_op jit(solution)/shard_map/ppermute | solution.py:210
  57.9 1.8 %collective-permute-done.3.far_ref = bf16[5,3,128,128]{3,2,1,0:T(8,128)(2,1)S(1)} collective-permute-done((bf16[5,3,128,128]{3,2,1,0:T(8,128)(2,1)S(1)}, bf16[5,3,128,128]{3,2,1,0:T(8,128)(2,1)S(1)}, u32[]{:S(2)}, u32[]{:S(2)}) %collective-permute-start.3) | collective-permute-done | bytes 491552 | tf_op jit(solution)/shard_map/ppermute | solution.py:210
  59.7 1.9 %all-to-all-done.1 = bf16[64,24,256]{2,1,0:T(8,128)(2,1)S(1)} async-done(((bf16[64,24,256]{2,1,0:T(8,128)(2,1)}), bf16[64,24,256]{2,1,0:T(8,128)(2,1)S(1)}, u32[]{:S(2)}, u32[]{:S(2)}) %all-to-all-start.1) | async-done | bytes 786464 | tf_op jit(solution)/shard_map/all_to_all | solution.py:207
  61.6 0.0 copy-done
  61.6 2.5 %apply.1 = bf16[12,128,128]{2,1,0:T(8,128)(2,1)S(1)} custom-call(bf16[1536,256]{1,0:T(8,128)(2,1)S(1)} %bitcast.9, bf16[5,2,128,128]{3,2,1,0:T(8,128)(2,1)S(1)} %copy-done.1, bf16[5,2,128,128]{3,2,1,0:T(8,128)(2,1)S(1)} %collective-permute-done.1.left_b, bf16[5,6,128,128]{3,2,1,0:T(8,128)(2,1)S(1)} %copy-done, ...), custom_call_target="tpu_custom_call" | custom-call | flops 2000000000 | bytes 4194304 | tf_op jit(solution)/shard_map/apply/pallas_call | solution.py:159
  64.2 22.3 %all_to_all.27 = bf16[12,128,128]{2,1,0:T(8,128)(2,1)S(1)} all-to-all(bf16[12,128,128]{2,1,0:T(8,128)(2,1)S(1)} %apply.1), channel_id=1, replica_groups={{0,128,256,384},{385,257,129,1},{64,192,320,448},{449,321,193,65},{2,13..., dimensions={0} | all-to-all | bytes 786432 | tf_op jit(solution)/shard_map/all_to_all | solution.py:230
  86.5 0.1 reduce_sum.12
  86.5 14.6 %all_gather.3.data_ref = bf16[12,128,128]{2,1,0:T(8,128)(2,1)S(1)} all-gather(bf16[3,128,128]{2,1,0:T(8,128)(2,1)S(1)} %reduce_sum.12), channel_id=1, replica_groups={{0,128,256,384},{385,257,129,1},{64,192,320,448},{449,321,193,65},{2,13..., dimensions={0}, use_global_device_ids=true | all-gather | bytes 491520 | tf_op jit(solution)/shard_map/all_gather | solution.py:235
  101.1 4.0 %collective-permute-start.4 = (bf16[12,128,128]{2,1,0:T(8,128)(2,1)S(1)}, bf16[12,128,128]{2,1,0:T(8,128)(2,1)S(1)}, u32[]{:S(2)}, u32[]{:S(2)}) collective-permute-start(bf16[12,128,128]{2,1,0:T(8,128)(2,1)S(1)} %all_gather.3.data_ref), channel_id=1, source_target_pairs={{0,64},{64,0},{1,65},{65,1},{2,66},{66,2},{3,67},{67,3},{4,68},{68... | collective-permute-start | bytes 1179656 | tf_op jit(solution)/shard_map/ppermute | solution.py:236
  105.1 0.8 place.2
  105.9 6.7 %collective-permute-done.4.data_ref = bf16[12,128,128]{2,1,0:T(8,128)(2,1)S(1)} collective-permute-done((bf16[12,128,128]{2,1,0:T(8,128)(2,1)S(1)}, bf16[12,128,128]{2,1,0:T(8,128)(2,1)S(1)}, u32[]{:S(2)}, u32[]{:S(2)}) %collective-permute-start.4) | collective-permute-done | bytes 393248 | tf_op jit(solution)/shard_map/ppermute | solution.py:236
  112.5 0.8 place.3
  (3 shorter events, 0.0 us)
Async XLA Ops:
  0.6 13.1 %copy-start.2 = (s32[1,768]{1,0:T(1,128)S(1)}, s32[1,768]{1,0:T(1,128)}, u32[]{:S(2)}) copy-start(s32[1,768]{1,0:T(1,128)} %param.9) | copy-start | bytes 9220
  0.6 17.4 %copy-start.1 = (bf16[5,2,128,128]{3,2,1,0:T(8,128)(2,1)S(1)}, bf16[5,2,128,128]{3,2,1,0:T(8,128)(2,1)}, u32[]{:S(2)}) copy-start(bf16[5,2,128,128]{3,2,1,0:T(8,128)(2,1)} %left_a.1) | copy-start | bytes 983044
  2.9 25.0 %all-to-all-start = ((bf16[64,24,128]{2,1,0:T(8,128)(2,1)}), bf16[64,24,128]{2,1,0:T(8,128)(2,1)S(1)}, u32[]{:S(2)}, u32[]{:S(2)}) async-start(bf16[64,24,128]{2,1,0:T(8,128)(2,1)} %bitcast.2), calls=%async_computation | async-start | bytes 786432 | tf_op jit(solution)/shard_map/all_to_all | solution.py:188
  13.7 6.4 %collective-permute-start = (s32[1,768]{1,0:T(1,128)S(1)}, s32[1,768]{1,0:T(1,128)S(1)}, u32[]{:S(2)}, u32[]{:S(2)}) collective-permute-start(s32[1,768]{1,0:T(1,128)S(1)} %copy-done.2), channel_id=1, source_target_pairs={{0,64},{64,0},{1,65},{65,1},{2,66},{66,2},{3,67},{67,3},{4,68},{68... | collective-permute-start | bytes 9224 | tf_op jit(solution)/shard_map/ppermute | solution.py:184
  18.0 11.7 %collective-permute-start.1 = (bf16[5,2,128,128]{3,2,1,0:T(8,128)(2,1)S(1)}, bf16[5,2,128,128]{3,2,1,0:T(8,128)(2,1)S(1)}, u32[]{:S(2)}, u32[]{:S(2)}) collective-permute-start(bf16[5,2,128,128]{3,2,1,0:T(8,128)(2,1)S(1)} %copy-done.1), channel_id=1, source_target_pairs={{0,64},{64,0},{1,65},{65,1},{2,66},{66,2},{3,67},{67,3},{4,68},{68... | collective-permute-start | bytes 983048 | tf_op jit(solution)/shard_map/ppermute | solution.py:189
  29.7 31.9 %copy-start = (bf16[5,6,128,128]{3,2,1,0:T(8,128)(2,1)S(1)}, bf16[5,6,128,128]{3,2,1,0:T(8,128)(2,1)}, u32[]{:S(2)}) copy-start(bf16[5,6,128,128]{3,2,1,0:T(8,128)(2,1)} %right_a.1) | copy-start | bytes 2949124
  29.8 31.9 %all-to-all-start.1 = ((bf16[64,24,256]{2,1,0:T(8,128)(2,1)}), bf16[64,24,256]{2,1,0:T(8,128)(2,1)S(1)}, u32[]{:S(2)}, u32[]{:S(2)}) async-start(bf16[64,24,256]{2,1,0:T(8,128)(2,1)} %bitcast.4), calls=%async_computation.1 | async-start | bytes 1572864 | tf_op jit(solution)/shard_map/all_to_all | solution.py:207
  40.8 15.2 %collective-permute-start.2 = (bf16[5,3,128,128]{3,2,1,0:T(8,128)(2,1)S(1)}, bf16[5,3,128,128]{3,2,1,0:T(8,128)(2,1)S(1)}, u32[]{:S(2)}, u32[]{:S(2)}) collective-permute-start(bf16[5,3,128,128]{3,2,1,0:T(8,128)(2,1)S(1)} %constant_dynamic-slice_fusion), channel_id=1, source_target_pairs={{0,64},{64,0},{1,65},{65,1},{2,66},{66,2},{3,67},{67,3},{4,68},{68... | collective-permute-start | bytes 1474568 | tf_op jit(solution)/shard_map/ppermute | solution.py:209
  56.0 3.7 %collective-permute-start.3 = (bf16[5,3,128,128]{3,2,1,0:T(8,128)(2,1)S(1)}, bf16[5,3,128,128]{3,2,1,0:T(8,128)(2,1)S(1)}, u32[]{:S(2)}, u32[]{:S(2)}) collective-permute-start(bf16[5,3,128,128]{3,2,1,0:T(8,128)(2,1)S(1)} %collective-permute-done.2.near_ref), channel_id=1, source_target_pairs={{0,1},{1,0},{2,3},{3,2},{4,5},{5,4},{6,7},{7,6},{8,9},{9,8},{10,11... | collective-permute-start | bytes 1474568 | tf_op jit(solution)/shard_map/ppermute | solution.py:210
  101.1 11.4 %collective-permute-start.4 = (bf16[12,128,128]{2,1,0:T(8,128)(2,1)S(1)}, bf16[12,128,128]{2,1,0:T(8,128)(2,1)S(1)}, u32[]{:S(2)}, u32[]{:S(2)}) collective-permute-start(bf16[12,128,128]{2,1,0:T(8,128)(2,1)S(1)} %all_gather.3.data_ref), channel_id=1, source_target_pairs={{0,64},{64,0},{1,65},{65,1},{2,66},{66,2},{3,67},{67,3},{4,68},{68... | collective-permute-start | bytes 1179656 | tf_op jit(solution)/shard_map/ppermute | solution.py:236
